TPU v7x, 32 devices: a whole 2x2x4 slice. The times are simulated.
32 devices in a mesh: mem: 4 (over x, core), lat: 4 (over z), lon: 2 (over y).
Axes of the slice: x: 2, y: 2, z: 4, core: 2. Of those that a mesh axis runs over, the one named last changes fastest.
Arguments:
- initial_temp: float32 [100, 8, 512], P(None, 'lon', 'lat'), may hold values from -6 to 6
- land_mask: int32 [8, 512], P('lon', 'lat'), may hold values 0 or 1
- pert_table: float32 [16, 100], replicated, may hold values from 0.03 to 0.24
- pert_index: int32 [8], P('mem'), may hold values from 0 to 15
- base_kh: float32 [100], replicated, may hold values from 0.03 to 0.24
- member_mix: bfloat16 [8, 100, 100], P('mem'), may hold values from -0.15625 to 0.15625
- base_mix: bfloat16 [100, 100], replicated, may hold values from -0.15625 to 0.15625
- owner: int32 [2048, 1], P(('lat', 'lon')), may hold values from 0 to 7; in each aligned block of 256 rows (0 to 255, 256 to 511, ...) at most 64 rows name the same one
- column: int32 [2048], P(('lat', 'lon')), may hold values from 0 to 511
- interp_w: float32 [2048, 100], P(('lat', 'lon')), may hold values from 0 to 1
- obs_inv_var: float32 [2048, 100], P(('lat', 'lon')), may hold values from 1 to 16
- observed: float32 [2048, 100], P(('lat', 'lon')), may hold values from -6 to 6
Outputs:
- member_temp: bfloat16 [8, 100, 8, 512], P('mem', None, 'lon', 'lat')
- base_temp: bfloat16 [100, 8, 512], P(None, 'lon', 'lat')
- gram_block: float32 [8, 8], replicated
- projection: float32 [8], replicated
- misfit: float32 [2048, 100], P(('lat', 'lon'))
Inputs may be any that keep to these rules, and one draw needn't show every extreme that they name: Within the records of one device no owner is named more than 64 times, and in every draw some owner is named exactly 64 times by some device's records. The column within the owner's block is the longitude offset times 128 plus the latitude offset.
All inputs are finite; a program needn't handle non-finite values. No bound on the sum of `land_mask` on one device may be relied on, other than what follows from the above.
Results may differ from a plain program's by a relative error of at most 0.012.
Values may be sent and summed in bfloat16 or wider, within the bound.
A program may use at most 64 MiB of HBM per device.

v0:
```python
import jax
import jax.numpy as jnp
from jax import lax
from jax.sharding import PartitionSpec as P

STEPS = 5


def padded_2(cells, sides, width, closed):
    for axis, dim in sides:
        count = lax.axis_size(axis)
        ends = count if closed else count - 1
        head = lax.slice_in_dim(cells, 0, width, axis=dim)
        tail = lax.slice_in_dim(cells, cells.shape[dim] - width, cells.shape[dim], axis=dim)
        cells = jnp.concatenate(
            [
                lax.ppermute(tail, axis, [(i, (i + 1) % count) for i in range(ends)]),
                cells,
                lax.ppermute(head, axis, [((i + 1) % count, i) for i in range(ends)]),
            ],
            axis=dim,
        )
    return cells


def on_device(
    initial_temp,
    land_mask,
    pert_table,
    pert_index,
    base_kh,
    member_mix,
    base_mix,
    owner,
    column,
    interp_w,
    obs_inv_var,
    observed,
):
    members = pert_index.shape[0]
    levels = initial_temp.shape[0]
    width_lon = initial_temp.shape[1]
    width_lat = initial_temp.shape[2]
    table_rows = pert_table.shape[0]
    chooser = (pert_index[:, None] == jnp.arange(table_rows)[None, :]).astype(jnp.float32)
    member_kh = jnp.dot(chooser, pert_table, precision=lax.Precision.HIGHEST)
    run_kh = jnp.concatenate([member_kh, base_kh[None, :]], 0)
    run_mix = jnp.concatenate([member_mix, base_mix[None]], 0)
    run_count = members + 1
    fields = jnp.broadcast_to(
        initial_temp.astype(jnp.bfloat16)[None], (run_count, levels, width_lon, width_lat)
    )
    total_lat = width_lat * lax.axis_size("lat")
    lat_start = lax.axis_index("lat") * width_lat
    ocean_open = land_mask.astype(jnp.float32)

    def advance(padded, open_cells, margin):
        global_rows = lat_start - (margin - 1) + jnp.arange(width_lat + 2 * (margin - 1))
        has_next = (global_rows < total_lat - 1).astype(jnp.float32)
        has_prior = (global_rows > 0).astype(jnp.float32)
        widened = padded.astype(jnp.float32)
        values = widened[:, :, 1:-1, 1:-1]
        laplace = widened[:, :, 2:, 1:-1] + widened[:, :, :-2, 1:-1] - 2.0 * values
        laplace = (
            laplace
            + has_next * (widened[:, :, 1:-1, 2:] - values)
            + has_prior * (widened[:, :, 1:-1, :-2] - values)
        )
        right_side = (values + run_kh[:, :, None, None] * laplace).astype(jnp.bfloat16)
        vertical = right_side.astype(jnp.float32) + jnp.einsum(
            "rkj,rjab->rkab", run_mix, right_side, preferred_element_type=jnp.float32
        )
        return (values + open_cells * (vertical - values)).astype(jnp.bfloat16)

    mask_wide = padded_2(land_mask, (("lon", 0),), 2, True)
    mask_full = padded_2(mask_wide, (("lat", 1),), 2, False).astype(jnp.float32)
    for step_index in range(0, STEPS, 2):
        lon_padded = padded_2(fields, (("lon", 2),), 2, True)
        padded = padded_2(lon_padded, (("lat", 3),), 2, False)
        halfway = advance(padded, mask_full[1:-1, 1:-1], 2)
        if step_index + 1 < STEPS:
            fields = advance(halfway, ocean_open, 1)
        else:
            fields = halfway[:, :, 1:-1, 1:-1]
    owners = lax.axis_size("lat") * lax.axis_size("lon")
    prof_dev = owner.shape[0]
    capacity = max(2, 2 * prof_dev // owners)
    target = owner[:, 0]
    matches = (target[:, None] == jnp.arange(owners)[None, :]).astype(jnp.int32)
    earlier = jnp.cumsum(matches, 0) - matches
    slot_rank = jnp.sum(earlier * matches, 1)
    position = target * capacity + slot_rank
    send_ids = (
        jnp.full((owners * capacity,), -1, jnp.int32)
        .at[position]
        .set(column)
        .reshape(owners, capacity)
    )
    records = jnp.stack([interp_w, obs_inv_var, observed], 1)
    send_records = (
        jnp.zeros((owners * capacity, 3, levels), jnp.float32)
        .at[position]
        .set(records)
        .reshape(owners, capacity, 3, levels)
    )
    columns_flat = fields.reshape(run_count, levels, width_lon * width_lat)
    column_ids = lax.all_to_all(send_ids, ("lat", "lon"), split_axis=0, concat_axis=0, tiled=True)
    record_rows = lax.all_to_all(
        send_records, ("lat", "lon"), split_axis=0, concat_axis=0, tiled=True
    )
    sources = column_ids.shape[0]
    slot_count = column_ids.shape[1]
    usable = (column_ids >= 0).astype(jnp.float32).reshape(-1)
    picked = jnp.take(columns_flat, jnp.maximum(column_ids, 0).reshape(-1), axis=2).astype(
        jnp.float32
    )
    deeper = jnp.concatenate([picked[:, 1:], picked[:, -1:]], 1)
    flat_records = record_rows.reshape(sources * slot_count, 3, levels)
    weight = flat_records[:, 0].T
    inv_var = flat_records[:, 1].T * usable
    measured = flat_records[:, 2].T
    modeled = weight * picked + (1.0 - weight) * deeper
    green_cols = ((modeled[:members] - modeled[members]) * usable).astype(jnp.bfloat16)
    misfit = (measured - modeled[members]) * usable
    extras = jnp.stack([inv_var, misfit], 0)
    green_cols, extras = (
        green_cols.reshape(members, levels, sources, slot_count),
        extras.reshape(2, levels, sources, slot_count),
    )
    owner_misfit = jnp.transpose(extras[1], (1, 2, 0))
    returned = lax.all_to_all(owner_misfit, ("lat", "lon"), split_axis=0, concat_axis=0, tiled=True)
    misfit_rows = jnp.take(returned.reshape(owners * capacity, levels), position, axis=0)
    green_cols = green_cols.reshape(members, levels, -1)
    extras = extras.reshape(2, levels, -1)
    normalizer = 1.0 / (prof_dev * owners * levels)
    green_all = lax.all_gather(green_cols, "mem", axis=0, tiled=True)
    green_float = green_all.astype(jnp.float32)
    weighted = green_float * extras[0]
    gram_part = (
        jnp.einsum("mks,nks->mn", weighted, green_float, precision=lax.Precision.HIGHEST)
        * normalizer
    )
    proj_part = (
        jnp.einsum("mks,ks->m", weighted, extras[1], precision=lax.Precision.HIGHEST) * normalizer
    )
    gram_part, proj_part = (gram_part, proj_part)
    gram_block, projection = lax.psum((gram_part, proj_part), ("lat", "lon"))
    return (fields[:members], fields[members], gram_block, projection, misfit_rows)


def solution(mesh):
    placed = (
        P(None, "lon", "lat"),
        P("lon", "lat"),
        P(),
        P("mem"),
        P(),
        P("mem", None, None),
        P(),
        P(("lat", "lon"), None),
        P(("lat", "lon")),
        P(("lat", "lon"), None),
        P(("lat", "lon"), None),
        P(("lat", "lon"), None),
    )
    return jax.shard_map(
        on_device,
        mesh=mesh,
        in_specs=placed,
        out_specs=(
            P("mem", None, "lon", "lat"),
            P(None, "lon", "lat"),
            P(),
            P(),
            P(("lat", "lon"), None),
        ),
        check_vma=False,
    )
```

profile of v0, /device:TPU:0, one launch (start us, length us, event | category | flops | bytes accessed | tf_op | source)
XLA Modules:
  0.0 144.0 jit_solution(2756762095311910528)
XLA Ops:
  2.0 3.0 %collective-permute-start.1 = (bf16[3,100,2,128]{1,3,2,0:T(8,128)(2,1)S(1)}, bf16[3,100,2,128]{1,3,2,0:T(8,128)(2,1)S(1)}, u32[]{:S(2)}, u32[]{:S(2)}) collective-permute-start(bf16[3,100,2,128]{1,3,2,0:T(8,128)(2,1)S(1)} %broadcast_in_dim.30), channel_id=1, source_target_pairs={{1,0},{0,1},{3,2},{2,3},{5,4},{4,5},{7,6},{6,7},{9,8},{8,9},{11,10... | collective-permute-start | bytes 460808 | tf_op jit(solution)/shard_map/ppermute | solution.py:19
  5.3 2.0 %collective-permute-start.5 = (s32[2,128]{1,0:T(2,128)S(1)}, s32[2,128]{1,0:T(2,128)S(1)}, u32[]{:S(2)}, u32[]{:S(2)}) collective-permute-start(s32[2,128]{1,0:T(2,128)S(1)} %get-tuple-element.39), channel_id=1, source_target_pairs={{1,0},{0,1},{3,2},{2,3},{5,4},{4,5},{7,6},{6,7},{9,8},{8,9},{11,10... | collective-permute-start | bytes 3080 | tf_op jit(solution)/shard_map/ppermute | solution.py:19
  11.1 6.2 %all-to-all-start.1 = ((s32[8,1,64]{2,1,0:T(1,128)}), s32[8,1,64]{2,1,0:T(1,128)S(1)}, u32[]{:S(2)}, u32[]{:S(2)}) async-start(s32[8,1,64]{2,1,0:T(1,128)} %all_to_all.13), calls=%async_computation.1 | async-start | bytes 8192 | tf_op jit(solution)/shard_map/all_to_all | solution.py:107
  19.2 4.5 %collective-permute-start.6 = (s32[8,2]{1,0:T(8,128)S(1)}, s32[8,2]{1,0:T(8,128)S(1)}, u32[]{:S(2)}, u32[]{:S(2)}) collective-permute-start(s32[8,2]{1,0:T(8,128)S(1)} %get-tuple-element.36), channel_id=1, source_target_pairs={{0,2},{2,4},{4,6},{1,3},{3,5},{5,7},{8,10},{10,12},{12,14},{9,11},... | collective-permute-start | bytes 200 | tf_op jit(solution)/shard_map/ppermute | solution.py:17
  25.2 4.6 %collective-permute-start.2 = (bf16[3,100,8,2]{1,3,2,0:T(2,128)(2,1)S(1)}, bf16[3,100,8,2]{1,3,2,0:T(2,128)(2,1)S(1)}, u32[]{:S(2)}, u32[]{:S(2)}) collective-permute-start(bf16[3,100,8,2]{1,3,2,0:T(2,128)(2,1)S(1)} %get-tuple-element.28), channel_id=1, source_target_pairs={{0,2},{2,4},{4,6},{1,3},{3,5},{5,7},{8,10},{10,12},{12,14},{9,11},... | collective-permute-start | bytes 28808 | tf_op jit(solution)/shard_map/ppermute | solution.py:17
  31.4 1.8 %fusion.17 = f32[3,100,6,130]{1,3,2,0:T(8,128)S(1)} fusion(f32[3,100,8,132]{1,3,2,0:T(8,128)S(1)} %maximum_convert_fusion, f32[130]{0:T(256)S(1)} %get-tuple-element.42, f32[130]{0:T(256)S(1)} %get-tuple-element.43, f32[3,100]{1,0:T(4,128)S(1)} %pad_maximum_fusion.10, f32[6,130]{1,0:T(8,128)S(1)} %fusion.121, bf16[1,100,100]{2,1,0:T(8,128)(2,1)S(1)} %bitcast.92, ...), kind=kOutput, calls=%fused_computation.25 | convolution fusion | flops 54174000 | bytes 13566016 | tf_op jit(solution)/shard_map/rkj,rjab->rkab/dot_general | solution.py:70
  34.4 2.1 %collective-permute-start.9 = (bf16[3,100,2,128]{1,3,2,0:T(8,128)(2,1)S(1)}, bf16[3,100,2,128]{1,3,2,0:T(8,128)(2,1)S(1)}, u32[]{:S(2)}, u32[]{:S(2)}) collective-permute-start(bf16[3,100,2,128]{1,3,2,0:T(8,128)(2,1)S(1)} %get-tuple-element.33), channel_id=1, source_target_pairs={{1,0},{0,1},{3,2},{2,3},{5,4},{4,5},{7,6},{6,7},{9,8},{8,9},{11,10... | collective-permute-start | bytes 460808 | tf_op jit(solution)/shard_map/ppermute | solution.py:19
  37.0 7.0 %scatter_fusion = f32[512,3,100]{2,1,0:T(4,128)S(1)} fusion(f32[512,3,100]{2,1,0:T(4,128)S(1)} %broadcast_in_dim.33, s32[256]{0:T(256)S(1)} %bitcast.88, f32[256,3,100]{2,1,0:T(4,128)S(1)} %copy.57), kind=kCustom, calls=%fused_computation.2 | custom fusion | bytes 922624 | tf_op jit(solution)/shard_map/scatter | solution.py:103
  46.4 4.8 %collective-permute-start.10 = (bf16[3,100,8,2]{1,3,2,0:T(2,128)(2,1)S(1)}, bf16[3,100,8,2]{1,3,2,0:T(2,128)(2,1)S(1)}, u32[]{:S(2)}, u32[]{:S(2)}) collective-permute-start(bf16[3,100,8,2]{1,3,2,0:T(2,128)(2,1)S(1)} %get-tuple-element.26), channel_id=1, source_target_pairs={{0,2},{2,4},{4,6},{1,3},{3,5},{5,7},{8,10},{10,12},{12,14},{9,11},... | collective-permute-start | bytes 28808 | tf_op jit(solution)/shard_map/ppermute | solution.py:17
  51.2 5.6 %all-to-all-start = ((f32[8,64,3,100]{3,1,2,0:T(8,128)}), f32[8,64,3,100]{3,1,2,0:T(8,128)S(1)}, u32[]{:S(2)}, u32[]{:S(2)}) async-start(f32[8,64,3,100]{3,1,2,0:T(8,128)} %copy.59), calls=%async_computation | async-start | bytes 1572864 | tf_op jit(solution)/shard_map/all_to_all | solution.py:108
  57.1 1.8 %fusion.15 = f32[3,100,6,130]{1,3,2,0:T(8,128)S(1)} fusion(f32[3,100,8,132]{1,3,2,0:T(8,128)S(1)} %maximum_convert_fusion.1, f32[130]{0:T(256)S(1)} %get-tuple-element.42, f32[130]{0:T(256)S(1)} %get-tuple-element.43, f32[3,100]{1,0:T(4,128)S(1)} %pad_maximum_fusion.10, f32[6,130]{1,0:T(8,128)S(1)} %fusion.121, bf16[1,100,100]{2,1,0:T(8,128)(2,1)S(1)} %bitcast.94, ...), kind=kOutput, calls=%fused_computation.23 | convolution fusion | flops 54174000 | bytes 13566016 | tf_op jit(solution)/shard_map/rkj,rjab->rkab/dot_general | solution.py:70
  60.1 2.1 %collective-permute-start.13 = (bf16[3,100,2,128]{1,3,2,0:T(8,128)(2,1)S(1)}, bf16[3,100,2,128]{1,3,2,0:T(8,128)(2,1)S(1)}, u32[]{:S(2)}, u32[]{:S(2)}) collective-permute-start(bf16[3,100,2,128]{1,3,2,0:T(8,128)(2,1)S(1)} %get-tuple-element.31), channel_id=1, source_target_pairs={{1,0},{0,1},{3,2},{2,3},{5,4},{4,5},{7,6},{6,7},{9,8},{8,9},{11,10... | collective-permute-start | bytes 460808 | tf_op jit(solution)/shard_map/ppermute | solution.py:19
  62.4 7.6 %collective-permute-done.13 = bf16[3,100,2,128]{1,3,2,0:T(8,128)(2,1)S(1)} collective-permute-done((bf16[3,100,2,128]{1,3,2,0:T(8,128)(2,1)S(1)}, bf16[3,100,2,128]{1,3,2,0:T(8,128)(2,1)S(1)}, u32[]{:S(2)}, u32[]{:S(2)}) %collective-permute-start.13) | collective-permute-done | bytes 153632 | tf_op jit(solution)/shard_map/ppermute | solution.py:19
  70.0 2.1 %collective-permute-done.12 = bf16[3,100,2,128]{1,3,2,0:T(8,128)(2,1)S(1)} collective-permute-done((bf16[3,100,2,128]{1,3,2,0:T(8,128)(2,1)S(1)}, bf16[3,100,2,128]{1,3,2,0:T(8,128)(2,1)S(1)}, u32[]{:S(2)}, u32[]{:S(2)}) %collective-permute-start.12) | collective-permute-done | bytes 153632 | tf_op jit(solution)/shard_map/ppermute | solution.py:17
  73.4 4.7 %collective-permute-start.14 = (bf16[3,100,8,2]{1,3,2,0:T(2,128)(2,1)S(1)}, bf16[3,100,8,2]{1,3,2,0:T(2,128)(2,1)S(1)}, u32[]{:S(2)}, u32[]{:S(2)}) collective-permute-start(bf16[3,100,8,2]{1,3,2,0:T(2,128)(2,1)S(1)} %get-tuple-element.24), channel_id=1, source_target_pairs={{0,2},{2,4},{4,6},{1,3},{3,5},{5,7},{8,10},{10,12},{12,14},{9,11},... | collective-permute-start | bytes 28808 | tf_op jit(solution)/shard_map/ppermute | solution.py:17
  79.6 1.9 %fusion.13 = bf16[3,100,6,130]{1,3,2,0:T(8,128)(2,1)S(1)} fusion(f32[3,100,8,132]{1,3,2,0:T(8,128)S(1)} %maximum_convert_fusion.2, f32[130]{0:T(256)S(1)} %get-tuple-element.42, f32[130]{0:T(256)S(1)} %get-tuple-element.43, f32[3,100]{1,0:T(4,128)S(1)} %pad_maximum_fusion.10, f32[6,130]{1,0:T(8,128)S(1)} %fusion.121, bf16[1,100,100]{2,1,0:T(8,128)(2,1)S(1)} %bitcast.96, ...), kind=kOutput, calls=%fused_computation.21 | convolution fusion | flops 53940000 | bytes 13098016 | tf_op jit(solution)/shard_map/rkj,rjab->rkab/dot_general | solution.py:70
  82.9 2.1 %gather_fusion = bf16[512,3,100]{2,1,0:T(4,128)(2,1)S(1)} fusion(bf16[3,100,512]{1,0,2:T(4,128)(2,1)S(1)} %copy.61, s32[1024]{0:T(1024)S(1)} %pad_clamp_fusion.1), kind=kCustom, calls=%fused_computation | custom fusion | bytes 616448 | tf_op jit(solution)/shard_map/jit(_take)/gather | solution.py:114
  88.0 1.8 %copy.66 = bf16[2,100,4,128]{3,2,1,0:T(4,128)(2,1)} copy(bf16[2,100,4,128]{1,3,2,0:T(8,128)(2,1)} %slice.260) | data formatting | bytes 409600
  92.2 1.9 %fusion.71 = f32[3,100,512]{1,0,2:T(4,128)S(1)} fusion(f32[3,1,512]{1,0,2:T(4,128)S(1)} %slice.266, f32[3,99,512]{1,0,2:T(4,128)S(1)} %slice.265, f32[100,512]{0,1:T(8,128)S(1)} %broadcast_subtract_fusion, f32[100,512]{0,1:T(8,128)S(1)} %slice_bitcast_fusion.2, bf16[512,3,100]{2,1,0:T(4,128)(2,1)S(1)} %gather_fusion, pred[512]{0:T(512)(128)(4,1)S(1)} %copy-done.9), kind=kLoop, calls=%fused_computation.80 | loop fusion | flops 921600 | bytes 1946112 | tf_op jit(solution)/shard_map/add | solution.py:122
  97.0 8.9 %all_gather.3 = bf16[8,100,512]{2,1,0:T(8,128)(2,1)S(1)} all-gather(bf16[2,100,512]{2,1,0:T(8,128)(2,1)S(1)} %copy.62), channel_id=1, replica_groups=mesh['mem'=4,'lat'=4,'lon'=2] {'mem'}, dimensions={0}, use_global_device_ids=true | all-gather | bytes 1024000 | tf_op jit(solution)/shard_map/all_gather | solution.py:136
  107.2 5.8 %all-to-all-start.2 = ((f32[8,64,100]{2,1,0:T(8,128)}), f32[8,64,100]{2,1,0:T(8,128)S(1)}, u32[]{:S(2)}, u32[]{:S(2)}) async-start(f32[8,64,100]{2,1,0:T(8,128)} %bitcast.31), calls=%async_computation.2 | async-start | bytes 524288 | tf_op jit(solution)/shard_map/all_to_all | solution.py:131
  113.3 3.9 %fusion.68 = f32[8]{0:T(128)S(1)} fusion(f32[100,512,1]{1,2,0:T(1,128)S(1)} %copy.74, f32[8,100,512]{2,1,0:T(8,128)S(1)} %convert_multiply_fusion), kind=kOutput, calls=%fused_computation.78 | convolution fusion | flops 4915208 | bytes 1843232 | tf_op jit(solution)/shard_map/mks,ks->m/dot_general | solution.py:144
  117.2 2.6 %fusion.62 = f32[8,8]{1,0:T(8,128)S(1)} fusion(f32[8,100,512]{2,1,0:T(8,128)S(1)} %convert_multiply_fusion, bf16[8,100,512]{2,1,0:T(8,128)(2,1)S(1)} %all_gather.3), kind=kOutput, calls=%fused_computation.76 | convolution fusion | flops 39321664 | bytes 2457856 | tf_op jit(solution)/shard_map/mks,nks->mn/dot_general | solution.py:140
  119.7 22.7 %all-reduce = (f32[8,8]{1,0:T(8,128)}, f32[8]{0:T(128)}) all-reduce(f32[8,8]{1,0:T(8,128)S(1)} %fusion.62, f32[8]{0:T(128)S(1)} %fusion.68), channel_id=1, replica_groups=mesh['mem'=4,'lat'=4,'lon'=2] {'lat','lon'}, use_global_device_ids=true, to_apply=%region_5.6 | all-reduce | flops 72 | bytes 576 | tf_op jit(solution)/shard_map/psum | solution.py:147
  (124 shorter events, 31.2 us)
Async XLA Ops:
  0.6 16.7 %copy-start = (f32[16,100]{1,0:T(8,128)S(1)}, f32[16,100]{1,0:T(8,128)}, u32[]{:S(2)}) copy-start(f32[16,100]{1,0:T(8,128)} %param.14) | copy-start | bytes 19204
  0.7 16.7 %copy-start.13 = (s32[2]{0:T(128)S(1)}, s32[2]{0:T(128)}, u32[]{:S(2)}) copy-start(s32[2]{0:T(128)} %param.15) | copy-start | bytes 28
  0.7 16.9 %copy-start.11 = (f32[100]{0:T(128)S(1)}, f32[100]{0:T(128)}, u32[]{:S(2)}) copy-start(f32[100]{0:T(128)} %param.16) | copy-start | bytes 1204
  0.7 17.0 %copy-start.5 = (bf16[2,100,100]{2,0,1:T(2,128)(2,1)S(1)}, bf16[2,100,100]{2,0,1:T(2,128)(2,1)}, u32[]{:S(2)}) copy-start(bf16[2,100,100]{2,0,1:T(2,128)(2,1)} %param.17) | copy-start | bytes 120004
  2.0 21.7 %collective-permute-start.1 = (bf16[3,100,2,128]{1,3,2,0:T(8,128)(2,1)S(1)}, bf16[3,100,2,128]{1,3,2,0:T(8,128)(2,1)S(1)}, u32[]{:S(2)}, u32[]{:S(2)}) collective-permute-start(bf16[3,100,2,128]{1,3,2,0:T(8,128)(2,1)S(1)} %broadcast_in_dim.30), channel_id=1, source_target_pairs={{1,0},{0,1},{3,2},{2,3},{5,4},{4,5},{7,6},{6,7},{9,8},{8,9},{11,10... | collective-permute-start | bytes 460808 | tf_op jit(solution)/shard_map/ppermute | solution.py:19
  5.2 18.6 %collective-permute-start = (bf16[3,100,2,128]{1,3,2,0:T(8,128)(2,1)S(1)}, bf16[3,100,2,128]{1,3,2,0:T(8,128)(2,1)S(1)}, u32[]{:S(2)}, u32[]{:S(2)}) collective-permute-start(bf16[3,100,2,128]{1,3,2,0:T(8,128)(2,1)S(1)} %broadcast_in_dim.28), channel_id=1, source_target_pairs={{0,1},{1,0},{2,3},{3,2},{4,5},{5,4},{6,7},{7,6},{8,9},{9,8},{10,11... | collective-permute-start | bytes 460808 | tf_op jit(solution)/shard_map/ppermute | solution.py:17
  5.3 12.5 %collective-permute-start.5 = (s32[2,128]{1,0:T(2,128)S(1)}, s32[2,128]{1,0:T(2,128)S(1)}, u32[]{:S(2)}, u32[]{:S(2)}) collective-permute-start(s32[2,128]{1,0:T(2,128)S(1)} %get-tuple-element.39), channel_id=1, source_target_pairs={{1,0},{0,1},{3,2},{2,3},{5,4},{4,5},{7,6},{6,7},{9,8},{8,9},{11,10... | collective-permute-start | bytes 3080 | tf_op jit(solution)/shard_map/ppermute | solution.py:19
  7.3 10.5 %collective-permute-start.4 = (s32[2,128]{1,0:T(2,128)S(1)}, s32[2,128]{1,0:T(2,128)S(1)}, u32[]{:S(2)}, u32[]{:S(2)}) collective-permute-start(s32[2,128]{1,0:T(2,128)S(1)} %get-tuple-element.38), channel_id=1, source_target_pairs={{0,1},{1,0},{2,3},{3,2},{4,5},{5,4},{6,7},{7,6},{8,9},{9,8},{10,11... | collective-permute-start | bytes 3080 | tf_op jit(solution)/shard_map/ppermute | solution.py:17
  11.1 40.1 %all-to-all-start.1 = ((s32[8,1,64]{2,1,0:T(1,128)}), s32[8,1,64]{2,1,0:T(1,128)S(1)}, u32[]{:S(2)}, u32[]{:S(2)}) async-start(s32[8,1,64]{2,1,0:T(1,128)} %all_to_all.13), calls=%async_computation.1 | async-start | bytes 8192 | tf_op jit(solution)/shard_map/all_to_all | solution.py:107
  17.9 11.8 %collective-permute-start.7 = (s32[8,2]{1,0:T(8,128)S(1)}, s32[8,2]{1,0:T(8,128)S(1)}, u32[]{:S(2)}, u32[]{:S(2)}) collective-permute-start(s32[8,2]{1,0:T(8,128)S(1)} %get-tuple-element.37), channel_id=1, source_target_pairs={{2,0},{4,2},{6,4},{3,1},{5,3},{7,5},{10,8},{12,10},{14,12},{11,9},... | collective-permute-start | bytes 200 | tf_op jit(solution)/shard_map/ppermute | solution.py:19
  19.2 10.6 %collective-permute-start.6 = (s32[8,2]{1,0:T(8,128)S(1)}, s32[8,2]{1,0:T(8,128)S(1)}, u32[]{:S(2)}, u32[]{:S(2)}) collective-permute-start(s32[8,2]{1,0:T(8,128)S(1)} %get-tuple-element.36), channel_id=1, source_target_pairs={{0,2},{2,4},{4,6},{1,3},{3,5},{5,7},{8,10},{10,12},{12,14},{9,11},... | collective-permute-start | bytes 200 | tf_op jit(solution)/shard_map/ppermute | solution.py:17
  23.8 6.0 %collective-permute-start.3 = (bf16[3,100,8,2]{1,3,2,0:T(2,128)(2,1)S(1)}, bf16[3,100,8,2]{1,3,2,0:T(2,128)(2,1)S(1)}, u32[]{:S(2)}, u32[]{:S(2)}) collective-permute-start(bf16[3,100,8,2]{1,3,2,0:T(2,128)(2,1)S(1)} %get-tuple-element.29), channel_id=1, source_target_pairs={{2,0},{4,2},{6,4},{3,1},{5,3},{7,5},{10,8},{12,10},{14,12},{11,9},... | collective-permute-start | bytes 28808 | tf_op jit(solution)/shard_map/ppermute | solution.py:19
  25.2 5.9 %collective-permute-start.2 = (bf16[3,100,8,2]{1,3,2,0:T(2,128)(2,1)S(1)}, bf16[3,100,8,2]{1,3,2,0:T(2,128)(2,1)S(1)}, u32[]{:S(2)}, u32[]{:S(2)}) collective-permute-start(bf16[3,100,8,2]{1,3,2,0:T(2,128)(2,1)S(1)} %get-tuple-element.28), channel_id=1, source_target_pairs={{0,2},{2,4},{4,6},{1,3},{3,5},{5,7},{8,10},{10,12},{12,14},{9,11},... | collective-permute-start | bytes 28808 | tf_op jit(solution)/shard_map/ppermute | solution.py:17
  34.4 10.6 %collective-permute-start.9 = (bf16[3,100,2,128]{1,3,2,0:T(8,128)(2,1)S(1)}, bf16[3,100,2,128]{1,3,2,0:T(8,128)(2,1)S(1)}, u32[]{:S(2)}, u32[]{:S(2)}) collective-permute-start(bf16[3,100,2,128]{1,3,2,0:T(8,128)(2,1)S(1)} %get-tuple-element.33), channel_id=1, source_target_pairs={{1,0},{0,1},{3,2},{2,3},{5,4},{4,5},{7,6},{6,7},{9,8},{8,9},{11,10... | collective-permute-start | bytes 460808 | tf_op jit(solution)/shard_map/ppermute | solution.py:19
  36.5 8.5 %collective-permute-start.8 = (bf16[3,100,2,128]{1,3,2,0:T(8,128)(2,1)S(1)}, bf16[3,100,2,128]{1,3,2,0:T(8,128)(2,1)S(1)}, u32[]{:S(2)}, u32[]{:S(2)}) collective-permute-start(bf16[3,100,2,128]{1,3,2,0:T(8,128)(2,1)S(1)} %get-tuple-element.32), channel_id=1, source_target_pairs={{0,1},{1,0},{2,3},{3,2},{4,5},{5,4},{6,7},{7,6},{8,9},{9,8},{10,11... | collective-permute-start | bytes 460808 | tf_op jit(solution)/shard_map/ppermute | solution.py:17
  45.1 11.8 %collective-permute-start.11 = (bf16[3,100,8,2]{1,3,2,0:T(2,128)(2,1)S(1)}, bf16[3,100,8,2]{1,3,2,0:T(2,128)(2,1)S(1)}, u32[]{:S(2)}, u32[]{:S(2)}) collective-permute-start(bf16[3,100,8,2]{1,3,2,0:T(2,128)(2,1)S(1)} %get-tuple-element.27), channel_id=1, source_target_pairs={{2,0},{4,2},{6,4},{3,1},{5,3},{7,5},{10,8},{12,10},{14,12},{11,9},... | collective-permute-start | bytes 28808 | tf_op jit(solution)/shard_map/ppermute | solution.py:19
  46.4 10.5 %collective-permute-start.10 = (bf16[3,100,8,2]{1,3,2,0:T(2,128)(2,1)S(1)}, bf16[3,100,8,2]{1,3,2,0:T(2,128)(2,1)S(1)}, u32[]{:S(2)}, u32[]{:S(2)}) collective-permute-start(bf16[3,100,8,2]{1,3,2,0:T(2,128)(2,1)S(1)} %get-tuple-element.26), channel_id=1, source_target_pairs={{0,2},{2,4},{4,6},{1,3},{3,5},{5,7},{8,10},{10,12},{12,14},{9,11},... | collective-permute-start | bytes 28808 | tf_op jit(solution)/shard_map/ppermute | solution.py:17
  51.2 40.3 %all-to-all-start = ((f32[8,64,3,100]{3,1,2,0:T(8,128)}), f32[8,64,3,100]{3,1,2,0:T(8,128)S(1)}, u32[]{:S(2)}, u32[]{:S(2)}) async-start(f32[8,64,3,100]{3,1,2,0:T(8,128)} %copy.59), calls=%async_computation | async-start | bytes 1572864 | tf_op jit(solution)/shard_map/all_to_all | solution.py:108
  60.1 9.9 %collective-permute-start.13 = (bf16[3,100,2,128]{1,3,2,0:T(8,128)(2,1)S(1)}, bf16[3,100,2,128]{1,3,2,0:T(8,128)(2,1)S(1)}, u32[]{:S(2)}, u32[]{:S(2)}) collective-permute-start(bf16[3,100,2,128]{1,3,2,0:T(8,128)(2,1)S(1)} %get-tuple-element.31), channel_id=1, source_target_pairs={{1,0},{0,1},{3,2},{2,3},{5,4},{4,5},{7,6},{6,7},{9,8},{8,9},{11,10... | collective-permute-start | bytes 460808 | tf_op jit(solution)/shard_map/ppermute | solution.py:19
  62.2 9.9 %collective-permute-start.12 = (bf16[3,100,2,128]{1,3,2,0:T(8,128)(2,1)S(1)}, bf16[3,100,2,128]{1,3,2,0:T(8,128)(2,1)S(1)}, u32[]{:S(2)}, u32[]{:S(2)}) collective-permute-start(bf16[3,100,2,128]{1,3,2,0:T(8,128)(2,1)S(1)} %get-tuple-element.30), channel_id=1, source_target_pairs={{0,1},{1,0},{2,3},{3,2},{4,5},{5,4},{6,7},{7,6},{8,9},{9,8},{10,11... | collective-permute-start | bytes 460808 | tf_op jit(solution)/shard_map/ppermute | solution.py:17
  72.1 6.2 %collective-permute-start.15 = (bf16[3,100,8,2]{1,3,2,0:T(2,128)(2,1)S(1)}, bf16[3,100,8,2]{1,3,2,0:T(2,128)(2,1)S(1)}, u32[]{:S(2)}, u32[]{:S(2)}) collective-permute-start(bf16[3,100,8,2]{1,3,2,0:T(2,128)(2,1)S(1)} %get-tuple-element.25), channel_id=1, source_target_pairs={{2,0},{4,2},{6,4},{3,1},{5,3},{7,5},{10,8},{12,10},{14,12},{11,9},... | collective-permute-start | bytes 28808 | tf_op jit(solution)/shard_map/ppermute | solution.py:19
  73.4 5.9 %collective-permute-start.14 = (bf16[3,100,8,2]{1,3,2,0:T(2,128)(2,1)S(1)}, bf16[3,100,8,2]{1,3,2,0:T(2,128)(2,1)S(1)}, u32[]{:S(2)}, u32[]{:S(2)}) collective-permute-start(bf16[3,100,8,2]{1,3,2,0:T(2,128)(2,1)S(1)} %get-tuple-element.24), channel_id=1, source_target_pairs={{0,2},{2,4},{4,6},{1,3},{3,5},{5,7},{8,10},{10,12},{12,14},{9,11},... | collective-permute-start | bytes 28808 | tf_op jit(solution)/shard_map/ppermute | solution.py:17
  107.2 35.2 %all-to-all-start.2 = ((f32[8,64,100]{2,1,0:T(8,128)}), f32[8,64,100]{2,1,0:T(8,128)S(1)}, u32[]{:S(2)}, u32[]{:S(2)}) async-start(f32[8,64,100]{2,1,0:T(8,128)} %bitcast.31), calls=%async_computation.2 | async-start | bytes 524288 | tf_op jit(solution)/shard_map/all_to_all | solution.py:131
  117.2 26.0 %copy-start.10 = (pred[256]{0:T(512)(128)(4,1)S(1)}, pred[256]{0:T(512)(128)(4,1)}, u32[]{:S(2)}) copy-start(pred[256]{0:T(512)(128)(4,1)} %get-tuple-element.22) | copy-start | bytes 772
  (9 other events, 36.0 us)
where the time goes:
time: 145 us; the launch traced here: 144 us
  starting transfers between devices  51 us (35%)
  blocking collectives  31.6 us (22%)
  local copies, waits for them, and re-layouts  23.8 us (16%)
  matrix products  14.5 us (10%)
  waiting for transfers between devices  12 us (8%)
  other arithmetic  9.77 us (7%)
    psum x1, blocking collectives, on_device(): gram_block, projection = lax.psum((gram_part, proj_part), ('lat', 'lon'))  22.7 us
    ppermute x8, starting transfers between devices, padded_2(): lax.ppermute(tail, axis, [(i, (i + 1) % count) for i in range(ends)])  19 us
    ppermute x8, starting transfers between devices, padded_2(): lax.ppermute(head, axis, [((i + 1) % count, i) for i in range(ends)])  14.3 us
    all_gather x1, blocking collectives, on_device(): green_all = lax.all_gather(green_cols, 'mem', axis=0, tiled=True)  8.94 us
    dot_general x5, matrix products, advance(): jnp.einsum('rkj,rjab->rkab', run_mix, right_side, preferred_element_type=...  7.88 us
    ppermute x8, waiting for transfers between devices, padded_2(): lax.ppermute(head, axis, [((i + 1) % count, i) for i in range(ends)])  7.6 us
    scatter x1, local copies, waits for them, and re-layouts, on_device(): send_records = jnp.zeros((owners * capacity, 3, levels), jnp.float32).at[...  6.97 us
    all_to_all x1, starting transfers between devices, on_device(): lax.all_to_all(send_ids, ('lat', 'lon'), split_axis=0, concat_axis=0, til...  6.25 us
  transfers between devices with their start and end apart: 19, of which 4 were waited for; matrix products, arithmetic and copies ran while one was open for 26% of the time, Pallas kernels for 0%

commit v1 on v0

v1 whole, which is shorter than its diff:
```python
import functools

import jax
import jax.numpy as jnp
import numpy as np
from jax import lax
from jax.experimental import pallas as pl
from jax.experimental.pallas import tpu as pltpu
from jax.sharding import PartitionSpec as P

STEPS = 5
SIDE = 8
CELL = 2 * SIDE
MESH = pl.DeviceIdType.MESH
BF, F32, I32 = jnp.bfloat16, jnp.float32, jnp.int32


def up(value, multiple):
    return -(-value // multiple) * multiple


def offsets_of(lon_count, width):
    reach = -(-STEPS // width)
    if 2 * reach + 1 >= lon_count:
        return list(range(lon_count)), True
    return list(range(-reach, reach + 1)), False


def lat_blocks(columns, ring, length):
    per = 128 // CELL
    halo_tiles = -(-columns // per)
    total = columns + halo_tiles

    def where(col, lat):
        if 0 <= lat < length:
            return col * length + lat
        inside = lat + SIDE if lat < 0 else lat - length + SIDE
        return (columns + col // per) * 128 + (col % per) * CELL + inside

    matrix = {}

    def put(source, target, amount):
        key = (source // 128, target // 128)
        block = matrix.setdefault(key, np.zeros((128, 128), np.float32))
        block[source % 128, target % 128] += amount

    for col in range(columns):
        for lat in range(-SIDE, length + SIDE):
            target = where(col, lat)
            put(target, target, -4.0)
            for step in (-1, 1):
                if -SIDE <= lat + step < length + SIDE:
                    put(where(col, lat + step), target, 1.0)
                near = col + step
                if ring:
                    near %= columns
                if 0 <= near < columns and not 0 <= lat < length:
                    put(where(near, lat), target, 1.0)
    plans, stacked = [], []
    for tile in range(total):
        sources = [s for s in range(total) if (s, tile) in matrix]
        start = sum(b.shape[0] for b in stacked)
        stacked += [matrix[(s, tile)] for s in sources]
        plans.append((sources, start))
    return plans, np.concatenate(stacked, 0)


def coords(linear, lat_count, lon_count):
    plane = lat_count * lon_count
    rest = linear % plane
    return linear // plane, rest // lon_count, rest % lon_count


def exchange_kernel(
    sizes, main_ref, edge_ref, owner_ref, column_ref, near_ref, halo_ref, ids_ref,
    main_send, main_recv, halo_send, halo_recv, ids_send, ids_recv,
):
    lat_count, lon_count, offsets, slots = sizes
    owners = lat_count * lon_count
    lat, lon = lax.axis_index("lat"), lax.axis_index("lon")
    me = lat * lon_count + lon
    barrier = pltpu.get_barrier_semaphore()

    def place(d):
        ll = (me + d) % owners
        return {"lat": ll // lon_count, "lon": ll % lon_count}

    def greet(d, carry):
        pl.semaphore_signal(barrier, inc=1, device_id=place(d), device_id_type=MESH)
        return carry

    lax.fori_loop(1, owners, greet, 0)

    records = owner_ref.shape[1]
    target = owner_ref[...]
    match = (lax.broadcasted_iota(I32, (up(owners, 16), records), 0) == target).astype(BF)
    before = (
        lax.broadcasted_iota(I32, (records, records), 0)
        < lax.broadcasted_iota(I32, (records, records), 1)
    ).astype(BF)
    earlier = jnp.dot(match, before, preferred_element_type=F32)
    rank = jnp.sum(earlier * match.astype(F32), axis=0, keepdims=True)
    position = target.astype(F32) * slots + rank
    row = lax.broadcasted_iota(I32, (8, records), 0)
    ids_ref[me] = jnp.where(row == 0, position, column_ref[...].astype(F32) + 1.0)
    pl.semaphore_wait(barrier, owners - 1)

    copies = []
    near = 0
    for index, offset in enumerate(offsets):
        to_lon = (lon - offset + lon_count) % lon_count
        if offset != 0:
            copies.append(
                pltpu.make_async_remote_copy(
                    main_ref, near_ref.at[near], main_send.at[near], main_recv.at[near],
                    device_id={"lat": lat, "lon": to_lon}, device_id_type=MESH,
                )
            )
            near += 1
        for side, step in ((0, 1), (1, lat_count - 1)):
            copies.append(
                pltpu.make_async_remote_copy(
                    edge_ref, halo_ref.at[index, side],
                    halo_send.at[index, side], halo_recv.at[index, side],
                    device_id={"lat": (lat + step) % lat_count, "lon": to_lon},
                    device_id_type=MESH,
                )
            )
    for copy in copies:
        copy.start()

    def ids_copy(d):
        return pltpu.make_async_remote_copy(
            ids_ref.at[me], ids_ref.at[me], ids_send.at[d - 1], ids_recv.at[d - 1],
            device_id=place(d), device_id_type=MESH,
        )

    def send_ids(d, carry):
        ids_copy(d).start()
        return carry

    lax.fori_loop(1, owners, send_ids, 0)

    def wait_ids(d, carry):
        source = (me + owners - d) % owners
        ids_copy(d).wait_send()
        pltpu.make_async_remote_copy(
            ids_ref.at[source], ids_ref.at[source], ids_send.at[d - 1], ids_recv.at[d - 1],
            device_id=place(d), device_id_type=MESH,
        ).wait_recv()
        return carry

    lax.fori_loop(1, owners, wait_ids, 0)
    for copy in copies:
        copy.wait()


def steps_kernel(
    sizes, plans, pert_index, main_ref, near_ref, halo_ref, ids_ref, blocks_ref, table_ref,
    base_kh_ref, mix_ref, base_mix_ref, fields_ref, picks_ref, base_ref, v_ref, rs_ref, f_ref,
):
    lat_count, lon_count, offsets, ring, slots, mem_count = sizes
    owners = lat_count * lon_count
    lat = lax.axis_index("lat")
    me = lat * lon_count + lax.axis_index("lon")
    rows = main_ref.shape[0]
    levels = table_ref.shape[1]
    own = main_ref.shape[1]
    runs = mix_ref.shape[0] + 1
    columns = len(offsets) * (own // 128)
    total = len(plans)
    first = offsets.index(0) * own
    lane = lax.broadcasted_iota(I32, (1, 128), 1)

    near = 0
    for index, offset in enumerate(offsets):
        if offset == 0:
            block = main_ref[...]
        else:
            block = near_ref[near]
            near += 1
        for run in range(runs):
            v_ref[run * rows : (run + 1) * rows, index * own : (index + 1) * own] = block
    low = lane % CELL < SIDE
    lanes = own // 128 * CELL
    per = 128 // lanes
    for tile in range(total - columns):
        value = jnp.zeros((rows, 128), F32)
        for part in range(per):
            index = tile * per + part
            if index >= len(offsets):
                continue
            prior = jnp.where(lat > 0, halo_ref[index, 0].astype(F32), 0.0)
            later = jnp.where(lat < lat_count - 1, halo_ref[index, 1].astype(F32), 0.0)
            both = jnp.where(low, prior, later)
            if part:
                both = pltpu.roll(both, part * lanes, 1)
            value = jnp.where((lane >= part * lanes) & (lane < (part + 1) * lanes), both, value)
        at = (columns + tile) * 128
        for run in range(runs):
            v_ref[run * rows : (run + 1) * rows, at : at + 128] = value.astype(BF)

    tail = v_ref[levels // 16 * 16 : levels // 16 * 16 + 16, :].astype(F32)
    open_row = tail[levels % 16 : levels % 16 + 1, :]

    def column_of(row):
        eye = lax.broadcasted_iota(I32, (rows, levels), 0) == lax.broadcasted_iota(
            I32, (rows, levels), 1
        )
        return jnp.sum(jnp.where(eye, row, 0.0), axis=1, keepdims=True)

    kh = [column_of(table_ref[pl.ds(pert_index[r], 1), :]) for r in range(runs - 1)]
    kh = jnp.concatenate(kh + [column_of(base_kh_ref[...])], 0)
    at_start = jnp.where(lat == 0, 1.0, 0.0)
    at_end = jnp.where(lat == lat_count - 1, 1.0, 0.0)
    edge = jnp.where(lane == 0, at_start, 0.0) + jnp.where(lane == 127, at_end, 0.0)

    def step(number, carry):
        for tile in range(total):
            sources, start = plans[tile]
            left = jnp.concatenate([v_ref[:, s * 128 : (s + 1) * 128] for s in sources], 1)
            right = blocks_ref[start : start + 128 * len(sources), :]
            laplace = jnp.dot(left, right, preferred_element_type=F32)
            values = v_ref[:, tile * 128 : (tile + 1) * 128].astype(F32)
            if tile < columns:
                for shift in (-1, 1):
                    other = tile + shift
                    if ring:
                        other %= columns
                    if 0 <= other < columns:
                        laplace += v_ref[:, other * 128 : (other + 1) * 128].astype(F32)
                laplace += edge * values
            rs_ref[:, tile * 128 : (tile + 1) * 128] = (values + kh * laplace).astype(BF)
        for run in range(runs):
            mix = mix_ref[run] if run < runs - 1 else base_mix_ref[...]
            top = run * rows
            for start in range(0, total, 3):
                end = min(start + 3, total)
                part = slice(start * 128, end * 128)
                right_side = rs_ref[top : top + levels, part]
                vertical = right_side.astype(F32) + jnp.dot(
                    mix, right_side, preferred_element_type=F32
                )
                values = v_ref[top : top + levels, part].astype(F32)
                v_ref[top : top + levels, part] = jnp.where(
                    open_row[:, part] > 0.5, vertical, values
                ).astype(BF)
        return carry

    lax.fori_loop(0, STEPS, step, 0)

    f_ref[...] = jnp.zeros_like(f_ref)
    for run in range(runs):
        block = v_ref[run * rows : (run + 1) * rows, first : first + own]
        fields_ref[run] = block
        f_ref[run * 128 : run * 128 + rows, :] = block

    each = slots // mem_count
    records = ids_ref.shape[2]
    fields = f_ref[...]

    def pick(source, carry):
        known = ids_ref[source]
        slot = lax.broadcasted_iota(I32, (slots, records), 0) + me * slots
        chosen = jnp.where(slot.astype(F32) == known[0:1], known[1:2], 0.0)
        cell = jnp.sum(chosen, axis=1, keepdims=True) - 1.0
        lanes_own = lax.broadcasted_iota(I32, (slots, own), 1).astype(F32)
        hot = jnp.where(lanes_own == cell, 1.0, 0.0).astype(BF)
        got = lax.dot_general(
            hot, fields, (((1,), (1,)), ((), ())), preferred_element_type=F32
        ).astype(BF)
        for run in range(runs - 1):
            for j in range(mem_count):
                picks_ref[source, j, run] = got[
                    j * each : (j + 1) * each, run * 128 : (run + 1) * 128
                ]
        base_ref[source] = got[:, (runs - 1) * 128 :]
        return carry

    lax.fori_loop(0, owners, pick, 0)


def gram_kernel(
    sizes, picks_ref, base_ref, ids_ref, owner_ref, w_ref, inv_ref, obs_ref, sum_ref, misfit_ref,
    got_ref, base_got, tiles_ref, got_send, got_recv, base_send, base_recv, sum_send, sum_recv,
):
    mem_count, lat_count, lon_count, slots = sizes
    owners = lat_count * lon_count
    world = mem_count * owners
    mem = lax.axis_index("mem")
    lat, lon = lax.axis_index("lat"), lax.axis_index("lon")
    plane = lat * lon_count + lon
    me = mem * owners + plane
    barrier = pltpu.get_barrier_semaphore()
    records, levels = w_ref.shape
    each = slots // mem_count
    local = picks_ref.shape[2]
    members = local * mem_count

    def device(linear):
        where = coords(linear, lat_count, lon_count)
        return {"mem": where[0], "lat": where[1], "lon": where[2]}

    def greet(d, carry):
        pl.semaphore_signal(
            barrier, inc=1, device_id=device((me + d) % world), device_id_type=MESH
        )
        return carry

    lax.fori_loop(1, world, greet, 0)
    got_ref[me] = picks_ref[plane, mem]
    base_got[plane] = base_ref[plane]
    pl.semaphore_wait(barrier, world - 1)

    def got_copy(d, slot):
        to = (me + d) % world
        return pltpu.make_async_remote_copy(
            picks_ref.at[to % owners, to // owners], got_ref.at[slot],
            got_send.at[d - 1], got_recv.at[d - 1],
            device_id=device(to), device_id_type=MESH,
        )

    def base_copy(d, slot):
        to = (plane + d) % owners
        return pltpu.make_async_remote_copy(
            base_ref.at[to], base_got.at[slot], base_send.at[d - 1], base_recv.at[d - 1],
            device_id=device(mem * owners + to), device_id_type=MESH,
        )

    def start_base(d, carry):
        base_copy(d, plane).start()
        return carry

    def start_got(d, carry):
        got_copy(d, me).start()
        return carry

    lax.fori_loop(1, owners, start_base, 0)
    lax.fori_loop(1, world, start_got, 0)

    target = owner_ref[...]
    match = (lax.broadcasted_iota(I32, (records, up(owners, 128)), 1) == target).astype(BF)
    before = (
        lax.broadcasted_iota(I32, (records, records), 1)
        < lax.broadcasted_iota(I32, (records, records), 0)
    ).astype(BF)
    earlier = jnp.dot(before, match, preferred_element_type=F32)
    rank = jnp.sum(earlier * match.astype(F32), axis=1, keepdims=True)
    position = target.astype(F32) * slots + rank
    position_row = ids_ref[plane][0:1]
    group = 8 if owners % 8 == 0 else owners
    wide = group * each

    def slot_values(chunk):
        slot = (
            (lax.broadcasted_iota(I32, (group, each, records), 0) + chunk * group) * slots
            + lax.broadcasted_iota(I32, (group, each, records), 1)
            + mem * each
        ).reshape(wide, records)
        hot = jnp.where(slot.astype(F32) == position_row, 1.0, 0.0)
        return [
            jnp.dot(hot, ref[...], precision=lax.Precision.HIGHEST, preferred_element_type=F32)
            for ref in (w_ref, inv_ref, obs_ref)
        ]

    lane = lax.broadcasted_iota(I32, (1, 128), 1)

    def interpolated(value, weight):
        deeper = jnp.where(lane == levels - 1, value, pltpu.roll(value, 127, 1))
        return weight * value[:, :levels] + (1.0 - weight) * deeper[:, :levels]

    early = slot_values(0) if owners == group else None

    def wait_base(d, carry):
        base_copy(d, (plane + owners - d) % owners).wait()
        return carry

    lax.fori_loop(1, owners, wait_base, 0)

    def spread(chunk, total):
        cells = base_got[pl.ds(chunk * group, group)].reshape(group * slots, 128)
        at = lax.broadcasted_iota(I32, (records, group * slots), 1) + chunk * (group * slots)
        hot = jnp.where(at.astype(F32) == position, 1.0, 0.0).astype(BF)
        return total + jnp.dot(hot, cells, preferred_element_type=F32)

    picked = jnp.zeros((records, 128), F32)
    if owners == group:
        picked = spread(0, picked)
    else:
        picked = lax.fori_loop(0, owners // group, spread, picked)
    misfit_ref[...] = obs_ref[...] - interpolated(picked, w_ref[...])

    def wait_got(d, carry):
        got_copy(d, (me + world - d) % world).wait()
        return carry

    lax.fori_loop(1, world, wait_got, 0)

    def gram(chunk, total):
        weight, inv_var, measured = slot_values(chunk) if early is None else early
        base = base_got[pl.ds(chunk * group, group), pl.ds(mem * each, each)]
        base = interpolated(base.reshape(wide, 128).astype(F32), weight)
        others = []
        for m in range(members):
            start = (m // local) * owners + chunk * group
            cells = got_ref[pl.ds(start, group), m % local].reshape(wide, 128).astype(F32)
            green = interpolated(cells, weight) - base
            others.append(green.astype(BF).astype(F32))
        others.append(measured - base)
        lines = []
        for m in range(members):
            weighted = others[m] * inv_var
            for n in range(members + 1):
                if n < m:
                    lines.append(lines[n * 16 + m])
                else:
                    lines.append(jnp.sum(weighted * others[n], axis=0, keepdims=True))
            lines += [jnp.zeros((1, levels), F32)] * (16 - members - 1)
        return total + jnp.concatenate(lines, 0)

    total = jnp.zeros((members * 16, levels), F32)
    if owners == group:
        total = gram(0, total)
    else:
        total = lax.fori_loop(0, owners // group, gram, total)
    sums = jnp.sum(total, axis=1, keepdims=True)
    spot = lax.broadcasted_iota(I32, (members, 16, 128), 1) == lax.broadcasted_iota(
        I32, (members, 16, 128), 2
    )
    tile = jnp.sum(jnp.where(spot, sums.reshape(members, 16, 1), 0.0), axis=1)
    tiles_ref[me] = tile

    def sum_copy(d, slot):
        return pltpu.make_async_remote_copy(
            tiles_ref.at[slot], tiles_ref.at[slot], sum_send.at[d - 1], sum_recv.at[d - 1],
            device_id=device((me + d) % world), device_id_type=MESH,
        )

    def start_sum(d, carry):
        sum_copy(d, me).start()
        return carry

    def wait_sum(d, carry):
        sum_copy(d, me).wait_send()
        sum_copy(d, (me + world - d) % world).wait_recv()
        return carry

    lax.fori_loop(1, world, start_sum, 0)
    lax.fori_loop(1, world, wait_sum, 0)
    sum_ref[...] = jnp.sum(tiles_ref[...], axis=0) * (1.0 / (records * owners * levels))


def vmem(count):
    return [pl.BlockSpec(memory_space=pltpu.VMEM)] * count


def on_device(
    mesh, initial_temp, land_mask, pert_table, pert_index, base_kh, member_mix, base_mix, owner,
    column, interp_w, obs_inv_var, observed,
):
    mem_count, lat_count, lon_count = (mesh.shape[a] for a in ("mem", "lat", "lon"))
    owners, world = lat_count * lon_count, mem_count * lat_count * lon_count
    levels, width, length = initial_temp.shape
    local = member_mix.shape[0]
    runs, records = local + 1, owner.shape[0]
    rows = up(levels + 1, 16)
    capacity = max(2, 2 * records // owners)
    slots = up(capacity, 16 * mem_count)
    each = slots // mem_count
    offsets, ring = offsets_of(lon_count, width)
    columns = len(offsets) * width
    plans, blocks = lat_blocks(columns, ring, length)
    total = len(plans)
    own = width * length
    limit = pltpu.CompilerParams(vmem_limit_bytes=48 << 20)

    cells = jnp.concatenate(
        [
            initial_temp.astype(BF),
            land_mask.astype(BF)[None],
            jnp.zeros((rows - levels - 1, width, length), BF),
        ],
        0,
    )
    edge = jnp.concatenate([cells[:, :, length - SIDE :], cells[:, :, :SIDE]], 2)
    edge = edge.reshape(rows, width * CELL)
    edge = jnp.pad(edge, ((0, 0), (0, 128 - width * CELL)))
    main = cells.reshape(rows, own)

    dma = pltpu.SemaphoreType.DMA
    near_count = max(1, len(offsets) - 1)
    near, halo, ids = pl.pallas_call(
        functools.partial(exchange_kernel, (lat_count, lon_count, offsets, slots)),
        out_shape=(
            jax.ShapeDtypeStruct((near_count, rows, own), BF),
            jax.ShapeDtypeStruct((len(offsets), 2, rows, 128), BF),
            jax.ShapeDtypeStruct((owners, 8, records), F32),
        ),
        in_specs=vmem(4),
        out_specs=tuple(vmem(3)),
        scratch_shapes=[
            dma((near_count,)), dma((near_count,)),
            dma((len(offsets), 2)), dma((len(offsets), 2)),
            dma((owners - 1,)), dma((owners - 1,)),
        ],
        compiler_params=pltpu.CompilerParams(
            collective_id=0, has_side_effects=True, vmem_limit_bytes=48 << 20
        ),
    )(main, edge, owner.reshape(1, records), column.reshape(1, records))

    fields, picks, base = pl.pallas_call(
        functools.partial(
            steps_kernel, (lat_count, lon_count, offsets, ring, slots, mem_count), plans
        ),
        out_shape=(
            jax.ShapeDtypeStruct((runs, rows, own), BF),
            jax.ShapeDtypeStruct((owners, mem_count, local, each, 128), BF),
            jax.ShapeDtypeStruct((owners, slots, 128), BF),
        ),
        in_specs=[pl.BlockSpec(memory_space=pltpu.SMEM)] + vmem(9),
        out_specs=tuple(vmem(3)),
        scratch_shapes=[
            pltpu.VMEM((runs * rows, total * 128), BF),
            pltpu.VMEM((runs * rows, total * 128), BF),
            pltpu.VMEM((runs * 128, own), BF),
        ],
        compiler_params=limit,
    )(
        pert_index, main, near, halo, ids, jnp.asarray(blocks, BF), pert_table,
        base_kh.reshape(1, levels), member_mix, base_mix,
    )

    sums, misfit = pl.pallas_call(
        functools.partial(gram_kernel, (mem_count, lat_count, lon_count, slots)),
        out_shape=(
            jax.ShapeDtypeStruct((local * mem_count, 128), F32),
            jax.ShapeDtypeStruct((records, levels), F32),
        ),
        in_specs=vmem(7),
        out_specs=tuple(vmem(2)),
        scratch_shapes=[
            pltpu.VMEM((world, local, each, 128), BF),
            pltpu.VMEM((owners, slots, 128), BF),
            pltpu.VMEM((world, local * mem_count, 128), F32),
            dma((world - 1,)), dma((world - 1,)),
            dma((owners - 1,)), dma((owners - 1,)),
            dma((world - 1,)), dma((world - 1,)),
        ],
        compiler_params=pltpu.CompilerParams(
            collective_id=1, has_side_effects=True, vmem_limit_bytes=48 << 20
        ),
    )(picks, base, ids, owner, interp_w, obs_inv_var, observed)

    members = local * mem_count
    final = fields[:, :levels].reshape(runs, levels, width, length)
    return (final[:local], final[local], sums[:, :members], sums[:, members], misfit)


def solution(mesh):
    placed = (
        P(None, "lon", "lat"),
        P("lon", "lat"),
        P(),
        P("mem"),
        P(),
        P("mem", None, None),
        P(),
        P(("lat", "lon"), None),
        P(("lat", "lon")),
        P(("lat", "lon"), None),
        P(("lat", "lon"), None),
        P(("lat", "lon"), None),
    )
    return jax.shard_map(
        functools.partial(on_device, mesh),
        mesh=mesh,
        in_specs=placed,
        out_specs=(
            P("mem", None, "lon", "lat"),
            P(None, "lon", "lat"),
            P(),
            P(),
            P(("lat", "lon"), None),
        ),
        check_vma=False,
    )
```

time: 145 us -> 56.2 us (0.39)
  starting transfers between devices: 51 us -> 0 us
  Pallas kernels: 0 us -> 44.9 us
  blocking collectives: 31.6 us -> 0 us
  local copies, waits for them, and re-layouts: 23.8 us -> 8.21 us
  matrix products: 14.5 us -> 0 us
  waiting for transfers between devices: 12 us -> 0 us
  other arithmetic: 9.77 us -> 1.94 us
    pallas_call x0 -> x3, Pallas kernels: none -> 44.9 us  [the longest x1 22.8 us: on_device(): pl.pallas_call(functools.partial(gram_kernel, (mem_count, lat_count, lon_...]
    ppermute x16 -> x0, starting transfers between devices: 33.3 us -> none  [the longest x8 19 us: padded_2(): lax.ppermute(tail, axis, [(i, (i + 1) % count) for i in range(ends)])]
    psum x1 -> x0, blocking collectives: 22.7 us -> none  [on_device(): gram_block, projection = lax.psum((gram_part, proj_part), ('lat', 'lon'))]
    all_to_all x3 -> x0, starting transfers between devices: 17.7 us -> none  [the longest x1 6.25 us: on_device(): lax.all_to_all(send_ids, ('lat', 'lon'), split_axis=0, concat_axis=0, til...]
    dot_general x8 -> x0, matrix products: 14.5 us -> none  [the longest x5 7.88 us: advance(): jnp.einsum('rkj,rjab->rkab', run_mix, right_side, preferred_element_type=...]
    ppermute x16 -> x0, waiting for transfers between devices: 12 us -> none  [the longest x8 7.6 us: padded_2(): lax.ppermute(head, axis, [((i + 1) % count, i) for i in range(ends)])]
    all_gather x1 -> x0, blocking collectives: 8.94 us -> none  [on_device(): green_all = lax.all_gather(green_cols, 'mem', axis=0, tiled=True)]
    scatter x2 -> x0, local copies, waits for them, and re-layouts: 8.52 us -> none  [the longest x1 6.97 us: on_device(): send_records = jnp.zeros((owners * capacity, 3, levels), jnp.float32).at[...]
  transfers between devices with their start and end apart: 19 -> 0, of which waited for: 4 -> 0; matrix products, arithmetic and copies ran while one was open for 26% -> 0% of each run, Pallas kernels for 0% -> 0%
where the time goes in v1:
time: 56.2 us; the launch traced here: 55.9 us
  Pallas kernels  44.9 us (80%)
  local copies, waits for them, and re-layouts  8.21 us (15%)
  other arithmetic  1.94 us (3%)
  between operations  0.82 us (1%)
    pallas_call x1, Pallas kernels, on_device(): pl.pallas_call(functools.partial(gram_kernel, (mem_count, lat_count, lon_...  22.8 us
    pallas_call x1, Pallas kernels, on_device(): pl.pallas_call(functools.partial(exchange_kernel, (lat_count, lon_count,...  11.6 us
    pallas_call x1, Pallas kernels, on_device(): pl.pallas_call(functools.partial(steps_kernel, (lat_count, lon_count, off...  10.6 us
    unnamed x32, local copies, waits for them, and re-layouts  5.58 us

profile of v1, /device:TPU:0, one launch (start us, length us, event | category | flops | bytes accessed | tf_op | source)
XLA Modules:
  0.0 55.9 jit_solution(17996175270717008302)
XLA Ops:
  0.6 0.7 %convert_bitcast_fusion = (bf16[1,4,128]{2,1,0:T(4,128)(2,1)S(1)}, bf16[1,1,4,128]{3,2,1,0:T(4,128)(2,1)S(1)}) fusion(s32[4,128]{1,0:T(4,128)} %param.14), kind=kLoop, calls=%fused_computation.5 | loop fusion | flops 512 | bytes 4096 | tf_op jit(solution)/shard_map/broadcast_in_dim | solution.py:480
  1.3 1.0 %convert_element_type.8 = bf16[100,4,128]{2,1,0:T(4,128)(2,1)S(1)} convert(f32[100,4,128]{2,1,0:T(4,128)} %param.13) | non-fusion elementwise | flops 51200 | bytes 307200 | tf_op jit(solution)/shard_map/convert_element_type | solution.py:479
  2.5 0.1 maximum_maximum_fusion.main_ref
  2.6 0.2 maximum_maximum_fusion.1
  2.8 0.1 fusion
  3.0 0.1 copy.51
  3.1 0.1 copy.53
  3.2 0.6 %copy-done.4 = s32[256]{0:T(256)S(1)} copy-done((s32[256]{0:T(256)S(1)}, s32[256]{0:T(256)}, u32[]{:S(2)}) %copy-start.4) | copy-done | bytes 1048
  3.9 11.6 %shard_map.164 = (bf16[1,112,512]{2,1,0:T(8,128)(2,1)S(1)}, bf16[2,2,112,128]{3,2,1,0:T(8,128)(2,1)S(1)}, f32[8,8,256]{2,1,0:T(8,128)S(1)}) custom-call(bf16[112,512]{1,0:T(8,128)(2,1)S(1)} %maximum_maximum_fusion.main_ref, bf16[112,128]{1,0:T(8,128)(2,1)S(1)} %pad.4.edge_ref, s32[1,256]{1,0:T(1,128)S(1)} %bitcast.17, s32[1,256]{1,0:T(1,128)S(1)} %bitcast.18), custom_call_target="tpu_custom_call" | custom-call | tf_op jit(solution)/shard_map/pallas_call | solution.py:492
  15.6 0.7 %copy-done.1 = bf16[100,100]{1,0:T(8,128)(2,1)S(1)} copy-done((bf16[100,100]{1,0:T(8,128)(2,1)S(1)}, bf16[100,100]{1,0:T(8,128)(2,1)}, u32[]{:S(2)}) %copy-start.1) | copy-done | bytes 20024
  16.3 10.6 %shard_map.165 = (bf16[3,112,512]{2,1,0:T(8,128)(2,1)S(1)}, bf16[8,4,2,16,128]{4,3,2,1,0:T(8,128)(2,1)S(1)}, bf16[8,64,128]{2,1,0:T(8,128)(2,1)S(1)}) custom-call(s32[2]{0:T(128)S(1)} %copy-done.5, bf16[112,512]{1,0:T(8,128)(2,1)S(1)} %maximum_maximum_fusion.main_ref, bf16[1,112,512]{2,1,0:T(8,128)(2,1)S(1)} %get-tuple-element.13.near_ref, ...), custom_call_target="tpu_custom_call" | custom-call | tf_op jit(solution)/shard_map/pallas_call | solution.py:511
  26.9 0.7 %slice.28 = bf16[2,100,4,128]{3,2,1,0:T(4,128)(2,1)} reshape(bf16[2,100,512]{2,1,0:T(8,128)(2,1)S(1)} %slice.27) | data formatting | bytes 409600 | tf_op jit(solution)/shard_map/slice | solution.py:556
  27.6 0.7 %squeeze.6 = bf16[100,4,128]{2,1,0:T(4,128)(2,1)} reshape(bf16[1,100,512]{2,1,0:T(8,128)(2,1)S(1)} %slice.29) | data formatting | bytes 204800 | tf_op jit(solution)/shard_map/squeeze | solution.py:556
  28.3 0.1 copy.55.owner_ref
  28.4 0.8 %copy-done.7 = f32[256,100]{0,1:T(8,128)S(1)} copy-done((f32[256,100]{0,1:T(8,128)S(1)}, f32[256,100]{0,1:T(8,128)}, u32[]{:S(2)}) %copy-start.7) | copy-done | bytes 102424
  29.2 0.1 copy.56.w_ref
  29.3 0.8 %copy-done.8 = f32[256,100]{0,1:T(8,128)S(1)} copy-done((f32[256,100]{0,1:T(8,128)S(1)}, f32[256,100]{0,1:T(8,128)}, u32[]{:S(2)}) %copy-start.8) | copy-done | bytes 102424
  30.1 0.1 copy.57.inv_ref
  30.2 0.8 %copy-done.9 = f32[256,100]{0,1:T(8,128)S(1)} copy-done((f32[256,100]{0,1:T(8,128)S(1)}, f32[256,100]{0,1:T(8,128)}, u32[]{:S(2)}) %copy-start.9) | copy-done | bytes 102424
  31.0 0.1 copy.58.obs_ref
  31.1 22.8 %shard_map.166 = (f32[8,128]{1,0:T(8,128)S(1)}, f32[256,100]{1,0:T(8,128)S(1)}) custom-call(bf16[8,4,2,16,128]{4,3,2,1,0:T(8,128)(2,1)S(1)} %get-tuple-element.17.picks_ref, bf16[8,64,128]{2,1,0:T(8,128)(2,1)S(1)} %get-tuple-element.18.base_ref, f32[8,8,256]{2,1,0:T(8,128)S(1)} %get-tuple-element.15.ids_ref, s32[256,1]{1,0:T(8,128)S(1)} %copy.55.owner_ref, ...), custom_call_target="tpu_custom_call" | custom-call | tf_op jit(solution)/shard_map/pallas_call | solution.py:533
  53.9 0.7 %slice_reduce_fusion = f32[8]{0:T(128)} fusion(f32[8,128]{1,0:T(8,128)S(1)} %get-tuple-element.19), kind=kLoop, calls=%fused_computation.3 | loop fusion | bytes 64 | tf_op jit(solution)/shard_map/slice | solution.py:556
  54.6 0.7 %copy.59 = f32[256,100]{0,1:T(8,128)} copy(f32[256,100]{1,0:T(8,128)S(1)} %get-tuple-element.45) | data formatting | bytes 204800
  55.3 0.6 %copy.65 = f32[8,8]{1,0:T(8,128)} copy(f32[8,8]{1,0:T(8,128)S(1)} %bitcast.16) | data formatting | bytes 512
  (28 shorter events, 0.4 us)
Async XLA Ops:
  2.4 13.2 %copy-start = (bf16[3200,128]{1,0:T(8,128)(2,1)S(1)}, bf16[3200,128]{1,0:T(8,128)(2,1)}, u32[]{:S(2)}) copy-start(bf16[3200,128]{1,0:T(8,128)(2,1)} %constant.6.clone.blocks_ref) | copy-start | bytes 2457604
  3.2 0.7 %copy-start.4 = (s32[256]{0:T(256)S(1)}, s32[256]{0:T(256)}, u32[]{:S(2)}) copy-start(s32[256]{0:T(256)} %param.21) | copy-start | bytes 3076
  3.2 0.7 %copy-start.3 = (s32[256,1]{0,1:T(1,128)S(1)}, s32[256,1]{0,1:T(1,128)}, u32[]{:S(2)}) copy-start(s32[256,1]{0,1:T(1,128)} %param.20) | copy-start | bytes 3076
  3.9 11.6 %copy-start.10 = (bf16[2,100,100]{2,0,1:T(2,128)(2,1)S(1)}, bf16[2,100,100]{2,0,1:T(2,128)(2,1)}, u32[]{:S(2)}) copy-start(bf16[2,100,100]{2,0,1:T(2,128)(2,1)} %param.18) | copy-start | bytes 120004
  15.5 0.7 %copy-start.1 = (bf16[100,100]{1,0:T(8,128)(2,1)S(1)}, bf16[100,100]{1,0:T(8,128)(2,1)}, u32[]{:S(2)}) copy-start(bf16[100,100]{1,0:T(8,128)(2,1)} %base_mix_ref.1) | copy-start | bytes 60004
  15.5 0.7 %copy-start.2 = (f32[16,100]{1,0:T(8,128)S(1)}, f32[16,100]{1,0:T(8,128)}, u32[]{:S(2)}) copy-start(f32[16,100]{1,0:T(8,128)} %table_ref.1) | copy-start | bytes 19204
  15.6 0.7 %copy-start.5 = (s32[2]{0:T(128)S(1)}, s32[2]{0:T(128)}, u32[]{:S(2)}) copy-start(s32[2]{0:T(128)} %pert_index.1) | copy-start | bytes 28
  15.6 0.7 %copy-start.6 = (f32[100]{0:T(128)S(1)}, f32[100]{0:T(128)}, u32[]{:S(2)}) copy-start(f32[100]{0:T(128)} %param.17) | copy-start | bytes 1204
  28.3 0.9 %copy-start.7 = (f32[256,100]{0,1:T(8,128)S(1)}, f32[256,100]{0,1:T(8,128)}, u32[]{:S(2)}) copy-start(f32[256,100]{0,1:T(8,128)} %param.22) | copy-start | bytes 307204
  29.2 0.9 %copy-start.8 = (f32[256,100]{0,1:T(8,128)S(1)}, f32[256,100]{0,1:T(8,128)}, u32[]{:S(2)}) copy-start(f32[256,100]{0,1:T(8,128)} %param.23) | copy-start | bytes 307204
  30.1 0.9 %copy-start.9 = (f32[256,100]{0,1:T(8,128)S(1)}, f32[256,100]{0,1:T(8,128)}, u32[]{:S(2)}) copy-start(f32[256,100]{0,1:T(8,128)} %param.24) | copy-start | bytes 307204

commit v2 on v1

--- a/solution.py
+++ b/solution.py
@@ -65,31 +65,46 @@
     return plans, np.concatenate(stacked, 0)
 
 
-def coords(linear, lat_count, lon_count):
-    plane = lat_count * lon_count
-    rest = linear % plane
-    return linear // plane, rest // lon_count, rest % lon_count
+def group_of(axis_sizes):
+    lat_count, lon_count = axis_sizes
+    me = lax.axis_index("lat") * lon_count + lax.axis_index("lon")
+    return me, lambda ll: {"lat": ll // lon_count, "lon": ll % lon_count}
 
 
 def exchange_kernel(
-    sizes, main_ref, edge_ref, owner_ref, column_ref, near_ref, halo_ref, ids_ref,
-    main_send, main_recv, halo_send, halo_recv, ids_send, ids_recv,
+    sizes, field_ref, mask_ref, owner_ref, column_ref, w_ref, inv_ref, obs_ref,
+    main_ref, near_ref, halo_ref, got_ref, stage_ref, edge_ref, message_ref,
+    main_send, main_recv, halo_send, halo_recv, got_send, got_recv,
 ):
-    lat_count, lon_count, offsets, slots = sizes
+    lat_count, lon_count, offsets, slots, each = sizes
     owners = lat_count * lon_count
-    lat, lon = lax.axis_index("lat"), lax.axis_index("lon")
-    me = lat * lon_count + lon
+    lat, lon, mem = lax.axis_index("lat"), lax.axis_index("lon"), lax.axis_index("mem")
+    me, place = group_of((lat_count, lon_count))
     barrier = pltpu.get_barrier_semaphore()
 
-    def place(d):
-        ll = (me + d) % owners
-        return {"lat": ll // lon_count, "lon": ll % lon_count}
-
     def greet(d, carry):
-        pl.semaphore_signal(barrier, inc=1, device_id=place(d), device_id_type=MESH)
+        pl.semaphore_signal(
+            barrier, inc=1, device_id=place((me + d) % owners), device_id_type=MESH
+        )
         return carry
 
     lax.fori_loop(1, owners, greet, 0)
+
+    levels, width, length = field_ref.shape
+    rows = main_ref.shape[0]
+    stage_ref[levels // 8 * 8 :, :] = jnp.zeros((rows - levels // 8 * 8, width * length), F32)
+    lane = lax.broadcasted_iota(I32, (1, 128), 1)
+    for c in range(width):
+        stage_ref[:levels, c * length : (c + 1) * length] = field_ref[:, c, :]
+        stage_ref[levels : levels + 1, c * length : (c + 1) * length] = mask_ref[
+            c : c + 1, :
+        ].astype(F32)
+    edge = jnp.zeros((rows, 128), F32)
+    for c in range(width):
+        cells = stage_ref[:, c * length : (c + 1) * length]
+        main_ref[:, c * length : (c + 1) * length] = cells.astype(BF)
+        edge = jnp.where(lane // CELL == c, pltpu.roll(cells, c * CELL + SIDE, 1), edge)
+    edge_ref[...] = edge.astype(BF)
 
     records = owner_ref.shape[1]
     target = owner_ref[...]
@@ -101,8 +116,7 @@
     earlier = jnp.dot(match, before, preferred_element_type=F32)
     rank = jnp.sum(earlier * match.astype(F32), axis=0, keepdims=True)
     position = target.astype(F32) * slots + rank
-    row = lax.broadcasted_iota(I32, (8, records), 0)
-    ids_ref[me] = jnp.where(row == 0, position, column_ref[...].astype(F32) + 1.0)
+    cell = column_ref[...].astype(F32) + 1.0
     pl.semaphore_wait(barrier, owners - 1)
 
     copies = []
@@ -129,37 +143,63 @@
     for copy in copies:
         copy.start()
 
-    def ids_copy(d):
+    message_ref[...] = jnp.zeros_like(message_ref)
+    slot = (
+        lax.broadcasted_iota(I32, (owners, each, records), 0) * slots
+        + lax.broadcasted_iota(I32, (owners, each, records), 1)
+        + mem * each
+    ).reshape(owners * each, records)
+    hot = jnp.where(slot.astype(F32) == position, 1.0, 0.0)
+    for kind, ref in enumerate((w_ref, inv_ref, obs_ref)):
+        chosen = lax.dot_general(
+            hot, ref[...], (((1,), (1,)), ((), ())),
+            precision=lax.Precision.HIGHEST, preferred_element_type=F32,
+        )
+        message_ref[:, kind * each : (kind + 1) * each, :levels] = chosen.reshape(
+            owners, each, levels
+        )
+    lines = records // 128
+    row = lax.broadcasted_iota(I32, (8, 128), 0)
+    head = jnp.zeros((8, 128), F32)
+    for line in range(lines):
+        part = slice(line * 128, (line + 1) * 128)
+        head = jnp.where(row == line, position[:, part], head)
+        head = jnp.where(row == lines + line, cell[:, part], head)
+    message_ref[:, 3 * each :, :] = jnp.broadcast_to(head[None], (owners, 8, 128))
+    got_ref[me] = message_ref[me]
+
+    def got_copy(d, slot):
+        to = (me + d) % owners
         return pltpu.make_async_remote_copy(
-            ids_ref.at[me], ids_ref.at[me], ids_send.at[d - 1], ids_recv.at[d - 1],
-            device_id=place(d), device_id_type=MESH,
-        )
-
-    def send_ids(d, carry):
-        ids_copy(d).start()
-        return carry
-
-    lax.fori_loop(1, owners, send_ids, 0)
-
-    def wait_ids(d, carry):
-        source = (me + owners - d) % owners
-        ids_copy(d).wait_send()
-        pltpu.make_async_remote_copy(
-            ids_ref.at[source], ids_ref.at[source], ids_send.at[d - 1], ids_recv.at[d - 1],
-            device_id=place(d), device_id_type=MESH,
-        ).wait_recv()
-        return carry
-
-    lax.fori_loop(1, owners, wait_ids, 0)
+            message_ref.at[to], got_ref.at[slot], got_send.at[d - 1], got_recv.at[d - 1],
+            device_id=place(to), device_id_type=MESH,
+        )
+
+    def send(d, carry):
+        got_copy(d, me).start()
+        return carry
+
+    def wait(d, carry):
+        got_copy(d, (me + owners - d) % owners).wait()
+        return carry
+
+    lax.fori_loop(1, owners, send, 0)
+    lax.fori_loop(1, owners, wait, 0)
     for copy in copies:
         copy.wait()
+
+
+def lines_of(known, start, records):
+    lines = records // 128
+    rows = [known[start + i : start + i + 1] for i in range(2 * lines)]
+    return jnp.concatenate(rows[:lines], 1), jnp.concatenate(rows[lines:], 1)
 
 
 def steps_kernel(
     sizes, plans, pert_index, main_ref, near_ref, halo_ref, ids_ref, blocks_ref, table_ref,
     base_kh_ref, mix_ref, base_mix_ref, fields_ref, picks_ref, base_ref, v_ref, rs_ref, f_ref,
 ):
-    lat_count, lon_count, offsets, ring, slots, mem_count = sizes
+    lat_count, lon_count, offsets, ring, slots, mem_count, records = sizes
     owners = lat_count * lon_count
     lat = lax.axis_index("lat")
     me = lat * lon_count + lax.axis_index("lon")
@@ -256,13 +296,12 @@
         f_ref[run * 128 : run * 128 + rows, :] = block
 
     each = slots // mem_count
-    records = ids_ref.shape[2]
     fields = f_ref[...]
 
     def pick(source, carry):
-        known = ids_ref[source]
+        position, column = lines_of(ids_ref[source], 3 * each, records)
         slot = lax.broadcasted_iota(I32, (slots, records), 0) + me * slots
-        chosen = jnp.where(slot.astype(F32) == known[0:1], known[1:2], 0.0)
+        chosen = jnp.where(slot.astype(F32) == position, column, 0.0)
         cell = jnp.sum(chosen, axis=1, keepdims=True) - 1.0
         lanes_own = lax.broadcasted_iota(I32, (slots, own), 1).astype(F32)
         hot = jnp.where(lanes_own == cell, 1.0, 0.0).astype(BF)
@@ -271,7 +310,7 @@
         ).astype(BF)
         for run in range(runs - 1):
             for j in range(mem_count):
-                picks_ref[source, j, run] = got[
+                picks_ref[j, source, run] = got[
                     j * each : (j + 1) * each, run * 128 : (run + 1) * 128
                 ]
         base_ref[source] = got[:, (runs - 1) * 128 :]
@@ -281,129 +320,86 @@
 
 
 def gram_kernel(
-    sizes, picks_ref, base_ref, ids_ref, owner_ref, w_ref, inv_ref, obs_ref, sum_ref, misfit_ref,
-    got_ref, base_got, tiles_ref, got_send, got_recv, base_send, base_recv, sum_send, sum_recv,
+    sizes, picks_ref, base_ref, message_ref, w_ref, obs_ref, sum_ref, misfit_ref,
+    got_ref, base_got, near_ref, tiles_ref, got_send, got_recv, base_send, base_recv,
+    near_send, near_recv, sum_send, sum_recv,
 ):
     mem_count, lat_count, lon_count, slots = sizes
     owners = lat_count * lon_count
-    world = mem_count * owners
     mem = lax.axis_index("mem")
-    lat, lon = lax.axis_index("lat"), lax.axis_index("lon")
-    plane = lat * lon_count + lon
-    me = mem * owners + plane
+    plane, place = group_of((lat_count, lon_count))
     barrier = pltpu.get_barrier_semaphore()
-    records, levels = w_ref.shape
+    levels, records = w_ref.shape
     each = slots // mem_count
     local = picks_ref.shape[2]
     members = local * mem_count
 
-    def device(linear):
-        where = coords(linear, lat_count, lon_count)
-        return {"mem": where[0], "lat": where[1], "lon": where[2]}
-
     def greet(d, carry):
         pl.semaphore_signal(
-            barrier, inc=1, device_id=device((me + d) % world), device_id_type=MESH
-        )
-        return carry
-
-    lax.fori_loop(1, world, greet, 0)
-    got_ref[me] = picks_ref[plane, mem]
+            barrier, inc=1, device_id=place((plane + d) % owners), device_id_type=MESH
+        )
+        return carry
+
+    for d in range(1, mem_count):
+        pl.semaphore_signal(
+            barrier, inc=1, device_id={"mem": (mem + d) % mem_count}, device_id_type=MESH
+        )
+    lax.fori_loop(1, owners, greet, 0)
+    got_ref[mem] = picks_ref[mem]
     base_got[plane] = base_ref[plane]
-    pl.semaphore_wait(barrier, world - 1)
+    pl.semaphore_wait(barrier, owners - 1 + mem_count - 1)
+
+    def mem_copy(d, source, target, send, recv):
+        return pltpu.make_async_remote_copy(
+            source, target, send.at[d - 1], recv.at[d - 1],
+            device_id={"mem": (mem + d) % mem_count}, device_id_type=MESH,
+        )
+
+    def plane_copy(d, source, target, send, recv):
+        return pltpu.make_async_remote_copy(
+            source, target, send.at[d - 1], recv.at[d - 1],
+            device_id=place((plane + d) % owners), device_id_type=MESH,
+        )
 
     def got_copy(d, slot):
-        to = (me + d) % world
-        return pltpu.make_async_remote_copy(
-            picks_ref.at[to % owners, to // owners], got_ref.at[slot],
-            got_send.at[d - 1], got_recv.at[d - 1],
-            device_id=device(to), device_id_type=MESH,
-        )
+        to = (mem + d) % mem_count
+        return mem_copy(d, picks_ref.at[to], got_ref.at[slot], got_send, got_recv)
 
     def base_copy(d, slot):
         to = (plane + d) % owners
-        return pltpu.make_async_remote_copy(
-            base_ref.at[to], base_got.at[slot], base_send.at[d - 1], base_recv.at[d - 1],
-            device_id=device(mem * owners + to), device_id_type=MESH,
-        )
+        return plane_copy(d, base_ref.at[to], base_got.at[slot], base_send, base_recv)
+
+    for d in range(1, mem_count):
+        got_copy(d, mem).start()
 
     def start_base(d, carry):
         base_copy(d, plane).start()
         return carry
 
-    def start_got(d, carry):
-        got_copy(d, me).start()
-        return carry
-
     lax.fori_loop(1, owners, start_base, 0)
-    lax.fori_loop(1, world, start_got, 0)
-
-    target = owner_ref[...]
-    match = (lax.broadcasted_iota(I32, (records, up(owners, 128)), 1) == target).astype(BF)
-    before = (
-        lax.broadcasted_iota(I32, (records, records), 1)
-        < lax.broadcasted_iota(I32, (records, records), 0)
-    ).astype(BF)
-    earlier = jnp.dot(before, match, preferred_element_type=F32)
-    rank = jnp.sum(earlier * match.astype(F32), axis=1, keepdims=True)
-    position = target.astype(F32) * slots + rank
-    position_row = ids_ref[plane][0:1]
+
     group = 8 if owners % 8 == 0 else owners
     wide = group * each
-
-    def slot_values(chunk):
-        slot = (
-            (lax.broadcasted_iota(I32, (group, each, records), 0) + chunk * group) * slots
-            + lax.broadcasted_iota(I32, (group, each, records), 1)
-            + mem * each
-        ).reshape(wide, records)
-        hot = jnp.where(slot.astype(F32) == position_row, 1.0, 0.0)
-        return [
-            jnp.dot(hot, ref[...], precision=lax.Precision.HIGHEST, preferred_element_type=F32)
-            for ref in (w_ref, inv_ref, obs_ref)
-        ]
-
     lane = lax.broadcasted_iota(I32, (1, 128), 1)
 
     def interpolated(value, weight):
         deeper = jnp.where(lane == levels - 1, value, pltpu.roll(value, 127, 1))
-        return weight * value[:, :levels] + (1.0 - weight) * deeper[:, :levels]
-
-    early = slot_values(0) if owners == group else None
-
-    def wait_base(d, carry):
-        base_copy(d, (plane + owners - d) % owners).wait()
-        return carry
-
-    lax.fori_loop(1, owners, wait_base, 0)
-
-    def spread(chunk, total):
-        cells = base_got[pl.ds(chunk * group, group)].reshape(group * slots, 128)
-        at = lax.broadcasted_iota(I32, (records, group * slots), 1) + chunk * (group * slots)
-        hot = jnp.where(at.astype(F32) == position, 1.0, 0.0).astype(BF)
-        return total + jnp.dot(hot, cells, preferred_element_type=F32)
-
-    picked = jnp.zeros((records, 128), F32)
-    if owners == group:
-        picked = spread(0, picked)
-    else:
-        picked = lax.fori_loop(0, owners // group, spread, picked)
-    misfit_ref[...] = obs_ref[...] - interpolated(picked, w_ref[...])
-
-    def wait_got(d, carry):
-        got_copy(d, (me + world - d) % world).wait()
-        return carry
-
-    lax.fori_loop(1, world, wait_got, 0)
+        return weight * value + (1.0 - weight) * deeper
+
+    for d in range(1, mem_count):
+        got_copy(d, (mem + mem_count - d) % mem_count).wait()
 
     def gram(chunk, total):
-        weight, inv_var, measured = slot_values(chunk) if early is None else early
-        base = base_got[pl.ds(chunk * group, group), pl.ds(mem * each, each)]
+        at = pl.ds(chunk * group, group)
+        weight, inv_var, measured = (
+            message_ref[at, kind * each : (kind + 1) * each, :].reshape(wide, 128)
+            for kind in range(3)
+        )
+        base = base_ref[at, pl.ds(pl.multiple_of(mem * each, each), each)]
         base = interpolated(base.reshape(wide, 128).astype(F32), weight)
         others = []
         for m in range(members):
-            start = (m // local) * owners + chunk * group
-            cells = got_ref[pl.ds(start, group), m % local].reshape(wide, 128).astype(F32)
+            cells = got_ref[m // local, at, m % local].reshape(wide, 128).astype(F32)
             green = interpolated(cells, weight) - base
             others.append(green.astype(BF).astype(F32))
         others.append(measured - base)
@@ -415,10 +411,10 @@
                     lines.append(lines[n * 16 + m])
                 else:
                     lines.append(jnp.sum(weighted * others[n], axis=0, keepdims=True))
-            lines += [jnp.zeros((1, levels), F32)] * (16 - members - 1)
+            lines += [jnp.zeros((1, 128), F32)] * (16 - members - 1)
         return total + jnp.concatenate(lines, 0)
 
-    total = jnp.zeros((members * 16, levels), F32)
+    total = jnp.zeros((members * 16, 128), F32)
     if owners == group:
         total = gram(0, total)
     else:
@@ -427,26 +423,63 @@
     spot = lax.broadcasted_iota(I32, (members, 16, 128), 1) == lax.broadcasted_iota(
         I32, (members, 16, 128), 2
     )
-    tile = jnp.sum(jnp.where(spot, sums.reshape(members, 16, 1), 0.0), axis=1)
-    tiles_ref[me] = tile
+    near_ref[mem] = jnp.sum(jnp.where(spot, sums.reshape(members, 16, 1), 0.0), axis=1)
+
+    def near_copy(d, slot):
+        return mem_copy(d, near_ref.at[mem], near_ref.at[slot], near_send, near_recv)
+
+    for d in range(1, mem_count):
+        near_copy(d, mem).start()
+
+    def wait_base(d, carry):
+        base_copy(d, (plane + owners - d) % owners).wait()
+        return carry
+
+    lax.fori_loop(1, owners, wait_base, 0)
+    position, _ = lines_of(message_ref[plane], 3 * each, records)
+
+    def spread(chunk, total):
+        cells = base_got[pl.ds(chunk * group, group)].reshape(group * slots, 128)
+        at = lax.broadcasted_iota(I32, (group * slots, records), 0) + chunk * (group * slots)
+        hot = jnp.where(at.astype(F32) == position, 1.0, 0.0).astype(BF)
+        return total + lax.dot_general(
+            cells, hot, (((0,), (0,)), ((), ())), preferred_element_type=F32
+        )
+
+    def misfit():
+        picked = jnp.zeros((128, records), F32)
+        if owners == group:
+            picked = spread(0, picked)
+        else:
+            picked = lax.fori_loop(0, owners // group, spread, picked)
+        deeper = pltpu.roll(picked, 127, 0)
+        level = lax.broadcasted_iota(I32, (128, 1), 0)
+        deeper = jnp.where(level == levels - 1, picked, deeper)
+        weight = w_ref[...]
+        misfit_ref[...] = obs_ref[...] - (
+            weight * picked[:levels] + (1.0 - weight) * deeper[:levels]
+        )
+
+    for d in range(1, mem_count):
+        near_copy(d, mem).wait_send()
+        near_copy(d, (mem + mem_count - d) % mem_count).wait_recv()
+    tiles_ref[plane] = jnp.sum(near_ref[...], axis=0)
 
     def sum_copy(d, slot):
-        return pltpu.make_async_remote_copy(
-            tiles_ref.at[slot], tiles_ref.at[slot], sum_send.at[d - 1], sum_recv.at[d - 1],
-            device_id=device((me + d) % world), device_id_type=MESH,
-        )
+        return plane_copy(d, tiles_ref.at[plane], tiles_ref.at[slot], sum_send, sum_recv)
 
     def start_sum(d, carry):
-        sum_copy(d, me).start()
+        sum_copy(d, plane).start()
         return carry
 
     def wait_sum(d, carry):
-        sum_copy(d, me).wait_send()
-        sum_copy(d, (me + world - d) % world).wait_recv()
-        return carry
-
-    lax.fori_loop(1, world, start_sum, 0)
-    lax.fori_loop(1, world, wait_sum, 0)
+        sum_copy(d, plane).wait_send()
+        sum_copy(d, (plane + owners - d) % owners).wait_recv()
+        return carry
+
+    lax.fori_loop(1, owners, start_sum, 0)
+    misfit()
+    lax.fori_loop(1, owners, wait_sum, 0)
     sum_ref[...] = jnp.sum(tiles_ref[...], axis=0) * (1.0 / (records * owners * levels))
 
 
@@ -459,7 +492,7 @@
     column, interp_w, obs_inv_var, observed,
 ):
     mem_count, lat_count, lon_count = (mesh.shape[a] for a in ("mem", "lat", "lon"))
-    owners, world = lat_count * lon_count, mem_count * lat_count * lon_count
+    owners = lat_count * lon_count
     levels, width, length = initial_temp.shape
     local = member_mix.shape[0]
     runs, records = local + 1, owner.shape[0]
@@ -474,31 +507,23 @@
     own = width * length
     limit = pltpu.CompilerParams(vmem_limit_bytes=48 << 20)
 
-    cells = jnp.concatenate(
-        [
-            initial_temp.astype(BF),
-            land_mask.astype(BF)[None],
-            jnp.zeros((rows - levels - 1, width, length), BF),
-        ],
-        0,
-    )
-    edge = jnp.concatenate([cells[:, :, length - SIDE :], cells[:, :, :SIDE]], 2)
-    edge = edge.reshape(rows, width * CELL)
-    edge = jnp.pad(edge, ((0, 0), (0, 128 - width * CELL)))
-    main = cells.reshape(rows, own)
-
+    w, inv_var, measured = interp_w.T, obs_inv_var.T, observed.T
     dma = pltpu.SemaphoreType.DMA
     near_count = max(1, len(offsets) - 1)
-    near, halo, ids = pl.pallas_call(
-        functools.partial(exchange_kernel, (lat_count, lon_count, offsets, slots)),
+    main, near, halo, messages = pl.pallas_call(
+        functools.partial(exchange_kernel, (lat_count, lon_count, offsets, slots, each)),
         out_shape=(
+            jax.ShapeDtypeStruct((rows, own), BF),
             jax.ShapeDtypeStruct((near_count, rows, own), BF),
             jax.ShapeDtypeStruct((len(offsets), 2, rows, 128), BF),
-            jax.ShapeDtypeStruct((owners, 8, records), F32),
+            jax.ShapeDtypeStruct((owners, 3 * each + 8, 128), F32),
         ),
-        in_specs=vmem(4),
-        out_specs=tuple(vmem(3)),
+        in_specs=vmem(7),
+        out_specs=tuple(vmem(4)),
         scratch_shapes=[
+            pltpu.VMEM((rows, own), F32),
+            pltpu.VMEM((rows, 128), BF),
+            pltpu.VMEM((owners, 3 * each + 8, 128), F32),
             dma((near_count,)), dma((near_count,)),
             dma((len(offsets), 2)), dma((len(offsets), 2)),
             dma((owners - 1,)), dma((owners - 1,)),
@@ -506,15 +531,18 @@
         compiler_params=pltpu.CompilerParams(
             collective_id=0, has_side_effects=True, vmem_limit_bytes=48 << 20
         ),
-    )(main, edge, owner.reshape(1, records), column.reshape(1, records))
+    )(
+        initial_temp, land_mask, owner.reshape(1, records), column.reshape(1, records),
+        w, inv_var, measured,
+    )
 
     fields, picks, base = pl.pallas_call(
         functools.partial(
-            steps_kernel, (lat_count, lon_count, offsets, ring, slots, mem_count), plans
+            steps_kernel, (lat_count, lon_count, offsets, ring, slots, mem_count, records), plans
         ),
         out_shape=(
             jax.ShapeDtypeStruct((runs, rows, own), BF),
-            jax.ShapeDtypeStruct((owners, mem_count, local, each, 128), BF),
+            jax.ShapeDtypeStruct((mem_count, owners, local, each, 128), BF),
             jax.ShapeDtypeStruct((owners, slots, 128), BF),
         ),
         in_specs=[pl.BlockSpec(memory_space=pltpu.SMEM)] + vmem(9),
@@ -526,7 +554,7 @@
         ],
         compiler_params=limit,
     )(
-        pert_index, main, near, halo, ids, jnp.asarray(blocks, BF), pert_table,
+        pert_index, main, near, halo, messages, jnp.asarray(blocks, BF), pert_table,
         base_kh.reshape(1, levels), member_mix, base_mix,
     )
 
@@ -534,26 +562,28 @@
         functools.partial(gram_kernel, (mem_count, lat_count, lon_count, slots)),
         out_shape=(
             jax.ShapeDtypeStruct((local * mem_count, 128), F32),
-            jax.ShapeDtypeStruct((records, levels), F32),
+            jax.ShapeDtypeStruct((levels, records), F32),
         ),
-        in_specs=vmem(7),
+        in_specs=vmem(5),
         out_specs=tuple(vmem(2)),
         scratch_shapes=[
-            pltpu.VMEM((world, local, each, 128), BF),
+            pltpu.VMEM((mem_count, owners, local, each, 128), BF),
             pltpu.VMEM((owners, slots, 128), BF),
-            pltpu.VMEM((world, local * mem_count, 128), F32),
-            dma((world - 1,)), dma((world - 1,)),
+            pltpu.VMEM((mem_count, local * mem_count, 128), F32),
+            pltpu.VMEM((owners, local * mem_count, 128), F32),
+            dma((mem_count - 1,)), dma((mem_count - 1,)),
             dma((owners - 1,)), dma((owners - 1,)),
-            dma((world - 1,)), dma((world - 1,)),
+            dma((mem_count - 1,)), dma((mem_count - 1,)),
+            dma((owners - 1,)), dma((owners - 1,)),
         ],
         compiler_params=pltpu.CompilerParams(
             collective_id=1, has_side_effects=True, vmem_limit_bytes=48 << 20
         ),
-    )(picks, base, ids, owner, interp_w, obs_inv_var, observed)
+    )(picks, base, messages, w, measured)
 
     members = local * mem_count
     final = fields[:, :levels].reshape(runs, levels, width, length)
-    return (final[:local], final[local], sums[:, :members], sums[:, members], misfit)
+    return (final[:local], final[local], sums[:, :members], sums[:, members], misfit.T)
 
 
 def solution(mesh):

time: 56.2 us -> 49.4 us (0.88)
  Pallas kernels: 44.9 us -> 39.6 us
  other arithmetic: 1.94 us -> 0 us
    pallas_call x1, Pallas kernels: 22.8 us -> 15.4 us  [on_device(): pl.pallas_call(functools.partial(gram_kernel, (mem_count, lat_count, lon_...]
    pallas_call x1, Pallas kernels: 11.6 us -> 13.4 us  [on_device(): pl.pallas_call(functools.partial(exchange_kernel, (lat_count, lon_count,...]
    unnamed x32 -> x29, local copies, waits for them, and re-layouts: 5.58 us -> 6.63 us
    convert_element_type x1 -> x0, other arithmetic: 0.97 us -> none  [on_device(): initial_temp.astype(BF)]
    broadcast_in_dim x1 -> x0, other arithmetic: 0.69 us -> none  [on_device(): land_mask.astype(BF)[None]]
where the time goes in v2:
time: 49.4 us; the launch traced here: 49.1 us
  Pallas kernels  39.6 us (80%)
  local copies, waits for them, and re-layouts  8.75 us (18%)
  between operations  0.78 us (2%)
    pallas_call x1, Pallas kernels, on_device(): pl.pallas_call(functools.partial(gram_kernel, (mem_count, lat_count, lon_...  15.4 us
    pallas_call x1, Pallas kernels, on_device(): pl.pallas_call(functools.partial(exchange_kernel, (lat_count, lon_count,...  13.4 us
    pallas_call x1, Pallas kernels, on_device(): pl.pallas_call(functools.partial(steps_kernel, (lat_count, lon_count, off...  10.8 us
    unnamed x29, local copies, waits for them, and re-layouts  6.63 us

profile of v2, /device:TPU:0, one launch (start us, length us, event | category | flops | bytes accessed | tf_op | source)
XLA Modules:
  0.0 49.1 jit_solution(11999957259159107653)
XLA Ops:
  0.6 0.0 copy-start.1
  0.6 0.0 copy-start.8
  0.7 0.0 copy-start.9
  0.7 0.0 copy-start.10
  0.7 0.9 %copy.19.mix_ref = bf16[2,100,100]{2,1,0:T(8,128)(2,1)S(1)} copy(bf16[2,100,100]{2,0,1:T(2,128)(2,1)} %param.18) | data formatting | bytes 80000 | tf_op args[5]
  1.5 0.0 copy-done.8
  1.6 0.0 copy-done.9
  1.6 0.0 copy-start.2
  1.6 0.9 %copy-done.2 = f32[256,100]{0,1:T(8,128)S(1)} copy-done((f32[256,100]{0,1:T(8,128)S(1)}, f32[256,100]{0,1:T(8,128)}, u32[]{:S(2)}) %copy-start.2) | copy-done | bytes 102424
  2.5 0.9 %copy-done.4 = f32[100,4,128]{2,1,0:T(4,128)S(1)} copy-done((f32[100,4,128]{2,1,0:T(4,128)S(1)}, f32[100,4,128]{2,1,0:T(4,128)}, u32[]{:S(2)}) %copy-start.4) | copy-done | bytes 204824
  3.4 0.9 %copy-done.5 = f32[256,100]{0,1:T(8,128)S(1)} copy-done((f32[256,100]{0,1:T(8,128)S(1)}, f32[256,100]{0,1:T(8,128)}, u32[]{:S(2)}) %copy-start.5) | copy-done | bytes 102424
  4.3 13.4 %shard_map.164 = (bf16[112,512]{1,0:T(8,128)(2,1)S(1)}, bf16[1,112,512]{2,1,0:T(8,128)(2,1)S(1)}, bf16[2,2,112,128]{3,2,1,0:T(8,128)(2,1)S(1)}, f32[8,56,128]{2,1,0:T(8,128)S(1)}) custom-call(f32[100,4,128]{2,1,0:T(4,128)S(1)} %copy-done.4, s32[4,128]{1,0:T(4,128)S(1)} %copy-done.8, s32[1,256]{1,0:T(1,128)S(1)} %bitcast.15, s32[1,256]{1,0:T(1,128)S(1)} %bitcast.16, ...), custom_call_target="tpu_custom_call" | custom-call | tf_op jit(solution)/shard_map/pallas_call | solution.py:513
  17.7 0.0 copy-start.11
  17.7 0.0 copy-start.12
  17.7 0.6 %copy-done.11 = s32[2]{0:T(128)S(1)} copy-done((s32[2]{0:T(128)S(1)}, s32[2]{0:T(128)}, u32[]{:S(2)}) %copy-start.11) | copy-done | bytes 32
  18.3 0.0 copy-done.12
  18.3 1.1 %copy-done = bf16[3200,128]{1,0:T(8,128)(2,1)S(1)} copy-done((bf16[3200,128]{1,0:T(8,128)(2,1)S(1)}, bf16[3200,128]{1,0:T(8,128)(2,1)}, u32[]{:S(2)}) %copy-start) | copy-done | bytes 819224
  19.5 10.8 %shard_map.165 = (bf16[3,112,512]{2,1,0:T(8,128)(2,1)S(1)}, bf16[4,8,2,16,128]{4,3,2,1,0:T(8,128)(2,1)S(1)}, bf16[8,64,128]{2,1,0:T(8,128)(2,1)S(1)}) custom-call(s32[2]{0:T(128)S(1)} %copy-done.11, bf16[112,512]{1,0:T(8,128)(2,1)S(1)} %get-tuple-element.14.main_ref, bf16[1,112,512]{2,1,0:T(8,128)(2,1)S(1)} %get-tuple-element.15.near_ref, ...), custom_call_target="tpu_custom_call" | custom-call | tf_op jit(solution)/shard_map/pallas_call | solution.py:539
  30.3 15.4 %shard_map.166 = (f32[8,128]{1,0:T(8,128)S(1)}, f32[100,256]{1,0:T(8,128)S(1)}) custom-call(bf16[4,8,2,16,128]{4,3,2,1,0:T(8,128)(2,1)S(1)} %get-tuple-element.19.picks_ref, bf16[8,64,128]{2,1,0:T(8,128)(2,1)S(1)} %get-tuple-element.20.base_ref, f32[8,56,128]{2,1,0:T(8,128)S(1)} %get-tuple-element.17.ids_ref.message_ref, f32[100,256]{1,0:T(8,128)S(1)} %bitcast.9, ...), custom_call_target="tpu_custom_call" | custom-call | tf_op jit(solution)/shard_map/pallas_call | solution.py:561
  45.8 0.7 %slice_reduce_fusion = f32[8]{0:T(128)} fusion(f32[8,128]{1,0:T(8,128)S(1)} %get-tuple-element.21), kind=kLoop, calls=%fused_computation | loop fusion | bytes 64 | tf_op jit(solution)/shard_map/slice | solution.py:586
  46.5 0.7 %slice.20 = bf16[2,100,4,128]{3,2,1,0:T(4,128)(2,1)} reshape(bf16[2,100,512]{2,1,0:T(8,128)(2,1)S(1)} %slice.19) | data formatting | bytes 409600 | tf_op jit(solution)/shard_map/slice | solution.py:586
  47.2 0.7 %squeeze.6 = bf16[100,4,128]{2,1,0:T(4,128)(2,1)} reshape(bf16[1,100,512]{2,1,0:T(8,128)(2,1)S(1)} %slice.21) | data formatting | bytes 204800 | tf_op jit(solution)/shard_map/squeeze | solution.py:586
  47.9 0.6 %copy.22 = f32[8,8]{1,0:T(8,128)} copy(f32[8,8]{1,0:T(8,128)S(1)} %bitcast.14) | data formatting | bytes 512
  48.5 0.6 %copy.23 = f32[256,100]{0,1:T(8,128)} copy(f32[256,100]{0,1:T(8,128)S(1)} %bitcast.13) | data formatting | bytes 204800
  (13 shorter events, 0.0 us)
Async XLA Ops:
  0.6 0.9 %copy-start.1 = (f32[256,100]{0,1:T(8,128)S(1)}, f32[256,100]{0,1:T(8,128)}, u32[]{:S(2)}) copy-start(f32[256,100]{0,1:T(8,128)} %param.22) | copy-start | bytes 307204
  0.6 0.9 %copy-start.8 = (s32[4,128]{1,0:T(4,128)S(1)}, s32[4,128]{1,0:T(4,128)}, u32[]{:S(2)}) copy-start(s32[4,128]{1,0:T(4,128)} %mask_ref.1) | copy-start | bytes 6148
  0.7 0.9 %copy-start.9 = (s32[256,1]{0,1:T(1,128)S(1)}, s32[256,1]{0,1:T(1,128)}, u32[]{:S(2)}) copy-start(s32[256,1]{0,1:T(1,128)} %param.20) | copy-start | bytes 3076
  0.7 0.9 %copy-start.10 = (s32[256]{0:T(256)S(1)}, s32[256]{0:T(256)}, u32[]{:S(2)}) copy-start(s32[256]{0:T(256)} %param.21) | copy-start | bytes 3076
  1.6 0.9 %copy-start.2 = (f32[256,100]{0,1:T(8,128)S(1)}, f32[256,100]{0,1:T(8,128)}, u32[]{:S(2)}) copy-start(f32[256,100]{0,1:T(8,128)} %param.24) | copy-start | bytes 307204
  2.5 0.9 %copy-start.4 = (f32[100,4,128]{2,1,0:T(4,128)S(1)}, f32[100,4,128]{2,1,0:T(4,128)}, u32[]{:S(2)}) copy-start(f32[100,4,128]{2,1,0:T(4,128)} %field_ref.1) | copy-start | bytes 614404
  3.4 0.9 %copy-start.5 = (f32[256,100]{0,1:T(8,128)S(1)}, f32[256,100]{0,1:T(8,128)}, u32[]{:S(2)}) copy-start(f32[256,100]{0,1:T(8,128)} %param.23) | copy-start | bytes 307204
  4.3 13.4 %copy-start.6 = (bf16[100,100]{1,0:T(8,128)(2,1)S(1)}, bf16[100,100]{1,0:T(8,128)(2,1)}, u32[]{:S(2)}) copy-start(bf16[100,100]{1,0:T(8,128)(2,1)} %base_mix_ref.1) | copy-start | bytes 60004
  4.3 13.4 %copy-start.7 = (f32[16,100]{1,0:T(8,128)S(1)}, f32[16,100]{1,0:T(8,128)}, u32[]{:S(2)}) copy-start(f32[16,100]{1,0:T(8,128)} %table_ref.1) | copy-start | bytes 19204
  17.7 0.7 %copy-start.11 = (s32[2]{0:T(128)S(1)}, s32[2]{0:T(128)}, u32[]{:S(2)}) copy-start(s32[2]{0:T(128)} %pert_index.1) | copy-start | bytes 28
  17.7 0.7 %copy-start.12 = (f32[100]{0:T(128)S(1)}, f32[100]{0:T(128)}, u32[]{:S(2)}) copy-start(f32[100]{0:T(128)} %param.17) | copy-start | bytes 1204
  18.3 1.1 %copy-start = (bf16[3200,128]{1,0:T(8,128)(2,1)S(1)}, bf16[3200,128]{1,0:T(8,128)(2,1)}, u32[]{:S(2)}) copy-start(bf16[3200,128]{1,0:T(8,128)(2,1)} %constant.2.clone.blocks_ref) | copy-start | bytes 2457604
  19.5 10.8 %copy-start.3 = (f32[256,100]{0,1:T(8,128)S(1)}, f32[256,100]{0,1:T(8,128)}, u32[]{:S(2)}) copy-start(f32[256,100]{0,1:T(8,128)} %param.24) | copy-start | bytes 307204

commit v3 on v2

--- a/solution.py
+++ b/solution.py
@@ -72,15 +72,33 @@
 
 
 def exchange_kernel(
-    sizes, field_ref, mask_ref, owner_ref, column_ref, w_ref, inv_ref, obs_ref,
-    main_ref, near_ref, halo_ref, got_ref, stage_ref, edge_ref, message_ref,
-    main_send, main_recv, halo_send, halo_recv, got_send, got_recv,
+    sizes, *refs
+):
+    sources, refs = refs[:7], refs[7:]
+    main_ref, near_ref, halo_ref, got_ref, stage_ref, edge_ref, message_ref = refs[:7]
+    fetched, fetch_sem = refs[7:14], refs[14]
+    field_ref, mask_ref, owner_ref, column_ref, w_ref, inv_ref, obs_ref = fetched
+    exchange(sizes, sources, fetched, fetch_sem, field_ref, mask_ref, owner_ref, column_ref,
+        w_ref, inv_ref, obs_ref, main_ref, near_ref, halo_ref, got_ref, stage_ref, edge_ref,
+        message_ref, *refs[15:])
+
+
+def exchange(
+    sizes, sources, fetched, fetch_sem, field_ref, mask_ref, owner_ref, column_ref,
+    w_ref, inv_ref, obs_ref, main_ref, near_ref, halo_ref, got_ref, stage_ref, edge_ref,
+    message_ref, main_send, main_recv, halo_send, halo_recv, got_send, got_recv,
 ):
     lat_count, lon_count, offsets, slots, each = sizes
     owners = lat_count * lon_count
     lat, lon, mem = lax.axis_index("lat"), lax.axis_index("lon"), lax.axis_index("mem")
     me, place = group_of((lat_count, lon_count))
     barrier = pltpu.get_barrier_semaphore()
+    fetches = [
+        pltpu.make_async_copy(source, target, fetch_sem.at[i])
+        for i, (source, target) in enumerate(zip(sources, fetched))
+    ]
+    for fetch in fetches:
+        fetch.start()
 
     def greet(d, carry):
         pl.semaphore_signal(
@@ -94,6 +112,8 @@
     rows = main_ref.shape[0]
     stage_ref[levels // 8 * 8 :, :] = jnp.zeros((rows - levels // 8 * 8, width * length), F32)
     lane = lax.broadcasted_iota(I32, (1, 128), 1)
+    for fetch in fetches[:4]:
+        fetch.wait()
     for c in range(width):
         stage_ref[:levels, c * length : (c + 1) * length] = field_ref[:, c, :]
         stage_ref[levels : levels + 1, c * length : (c + 1) * length] = mask_ref[
@@ -116,7 +136,9 @@
     earlier = jnp.dot(match, before, preferred_element_type=F32)
     rank = jnp.sum(earlier * match.astype(F32), axis=0, keepdims=True)
     position = target.astype(F32) * slots + rank
-    cell = column_ref[...].astype(F32) + 1.0
+    spot, cell = position.astype(I32), column_ref[...] + 1
+    digits = [(n >> 6, n & 63) for n in (spot, cell)]
+    digits = [d.astype(F32) for pair in digits for d in pair]
     pl.semaphore_wait(barrier, owners - 1)
 
     copies = []
@@ -144,6 +166,8 @@
         copy.start()
 
     message_ref[...] = jnp.zeros_like(message_ref)
+    for fetch in fetches[4:]:
+        fetch.wait()
     slot = (
         lax.broadcasted_iota(I32, (owners, each, records), 0) * slots
         + lax.broadcasted_iota(I32, (owners, each, records), 1)
@@ -157,15 +181,15 @@
         )
         message_ref[:, kind * each : (kind + 1) * each, :levels] = chosen.reshape(
             owners, each, levels
-        )
+        ).astype(BF)
     lines = records // 128
-    row = lax.broadcasted_iota(I32, (8, 128), 0)
-    head = jnp.zeros((8, 128), F32)
+    row = lax.broadcasted_iota(I32, (16, 128), 0)
+    head = jnp.zeros((16, 128), F32)
     for line in range(lines):
         part = slice(line * 128, (line + 1) * 128)
-        head = jnp.where(row == line, position[:, part], head)
-        head = jnp.where(row == lines + line, cell[:, part], head)
-    message_ref[:, 3 * each :, :] = jnp.broadcast_to(head[None], (owners, 8, 128))
+        for kind, digit in enumerate(digits):
+            head = jnp.where(row == kind * lines + line, digit[:, part], head)
+    message_ref[:, 3 * each :, :] = jnp.broadcast_to(head.astype(BF)[None], (owners, 16, 128))
     got_ref[me] = message_ref[me]
 
     def got_copy(d, slot):
@@ -189,16 +213,30 @@
         copy.wait()
 
 
-def lines_of(known, start, records):
+def lines_of(known, records):
     lines = records // 128
-    rows = [known[start + i : start + i + 1] for i in range(2 * lines)]
-    return jnp.concatenate(rows[:lines], 1), jnp.concatenate(rows[lines:], 1)
+    digits = known.astype(F32)
+    rows = [digits[i : i + 1] for i in range(4 * lines)]
+    high, low, cell_high, cell_low = (
+        jnp.concatenate(rows[k * lines : (k + 1) * lines], 1) for k in range(4)
+    )
+    return high * 64.0 + low, cell_high * 64.0 + cell_low
 
 
 def steps_kernel(
-    sizes, plans, pert_index, main_ref, near_ref, halo_ref, ids_ref, blocks_ref, table_ref,
-    base_kh_ref, mix_ref, base_mix_ref, fields_ref, picks_ref, base_ref, v_ref, rs_ref, f_ref,
+    sizes, plans, pert_index, main_ref, near_ref, halo_ref, ids_ref, mix_ref, base_mix_ref,
+    blocks_at, table_at, base_kh_at, members_out, base_out, picks_ref, base_ref, v_ref, rs_ref,
+    f_ref, blocks_ref, table_ref, base_kh_ref, wide_ref, final_ref, fetch_sem,
+    out_sem,
 ):
+    fetches = [
+        pltpu.make_async_copy(source, target, fetch_sem.at[i])
+        for i, (source, target) in enumerate(
+            ((blocks_at, blocks_ref), (table_at, table_ref), (base_kh_at, base_kh_ref))
+        )
+    ]
+    for fetch in fetches:
+        fetch.start()
     lat_count, lon_count, offsets, ring, slots, mem_count, records = sizes
     owners = lat_count * lon_count
     lat = lax.axis_index("lat")
@@ -249,6 +287,8 @@
         )
         return jnp.sum(jnp.where(eye, row, 0.0), axis=1, keepdims=True)
 
+    for fetch in fetches:
+        fetch.wait()
     kh = [column_of(table_ref[pl.ds(pert_index[r], 1), :]) for r in range(runs - 1)]
     kh = jnp.concatenate(kh + [column_of(base_kh_ref[...])], 0)
     at_start = jnp.where(lat == 0, 1.0, 0.0)
@@ -292,14 +332,26 @@
     f_ref[...] = jnp.zeros_like(f_ref)
     for run in range(runs):
         block = v_ref[run * rows : (run + 1) * rows, first : first + own]
-        fields_ref[run] = block
         f_ref[run * 128 : run * 128 + rows, :] = block
+        length = 128
+        for c in range(own // length):
+            wide_ref[run, :, c, :] = block[:levels, c * length : (c + 1) * length].astype(F32)
+        final_ref[run] = wide_ref[run].astype(BF)
+    outs = [
+        pltpu.make_async_copy(
+            final_ref.at[run], members_out.at[run] if run < runs - 1 else base_out,
+            out_sem.at[run],
+        )
+        for run in range(runs)
+    ]
+    for out in outs:
+        out.start()
 
     each = slots // mem_count
     fields = f_ref[...]
 
     def pick(source, carry):
-        position, column = lines_of(ids_ref[source], 3 * each, records)
+        position, column = lines_of(ids_ref[source, 3 * each :], records)
         slot = lax.broadcasted_iota(I32, (slots, records), 0) + me * slots
         chosen = jnp.where(slot.astype(F32) == position, column, 0.0)
         cell = jnp.sum(chosen, axis=1, keepdims=True) - 1.0
@@ -317,11 +369,13 @@
         return carry
 
     lax.fori_loop(0, owners, pick, 0)
+    for out in outs:
+        out.wait()
 
 
 def gram_kernel(
-    sizes, picks_ref, base_ref, message_ref, w_ref, obs_ref, sum_ref, misfit_ref,
-    got_ref, base_got, near_ref, tiles_ref, got_send, got_recv, base_send, base_recv,
+    sizes, picks_ref, base_ref, message_ref, w_at, obs_at, sum_ref, misfit_ref,
+    w_ref, obs_ref, fetch_sem, got_ref, base_got, near_ref, tiles_ref, got_send, got_recv, base_send, base_recv,
     near_send, near_recv, sum_send, sum_recv,
 ):
     mem_count, lat_count, lon_count, slots = sizes
@@ -330,6 +384,12 @@
     plane, place = group_of((lat_count, lon_count))
     barrier = pltpu.get_barrier_semaphore()
     levels, records = w_ref.shape
+    fetches = [
+        pltpu.make_async_copy(w_at, w_ref, fetch_sem.at[0]),
+        pltpu.make_async_copy(obs_at, obs_ref, fetch_sem.at[1]),
+    ]
+    for fetch in fetches:
+        fetch.start()
     each = slots // mem_count
     local = picks_ref.shape[2]
     members = local * mem_count
@@ -392,7 +452,7 @@
     def gram(chunk, total):
         at = pl.ds(chunk * group, group)
         weight, inv_var, measured = (
-            message_ref[at, kind * each : (kind + 1) * each, :].reshape(wide, 128)
+            message_ref[at, kind * each : (kind + 1) * each, :].reshape(wide, 128).astype(F32)
             for kind in range(3)
         )
         base = base_ref[at, pl.ds(pl.multiple_of(mem * each, each), each)]
@@ -436,7 +496,7 @@
         return carry
 
     lax.fori_loop(1, owners, wait_base, 0)
-    position, _ = lines_of(message_ref[plane], 3 * each, records)
+    position, _ = lines_of(message_ref[plane, 3 * each :], records)
 
     def spread(chunk, total):
         cells = base_got[pl.ds(chunk * group, group)].reshape(group * slots, 128)
@@ -455,6 +515,8 @@
         deeper = pltpu.roll(picked, 127, 0)
         level = lax.broadcasted_iota(I32, (128, 1), 0)
         deeper = jnp.where(level == levels - 1, picked, deeper)
+        for fetch in fetches:
+            fetch.wait()
         weight = w_ref[...]
         misfit_ref[...] = obs_ref[...] - (
             weight * picked[:levels] + (1.0 - weight) * deeper[:levels]
@@ -481,6 +543,33 @@
     misfit()
     lax.fori_loop(1, owners, wait_sum, 0)
     sum_ref[...] = jnp.sum(tiles_ref[...], axis=0) * (1.0 / (records * owners * levels))
+
+
+def last_kernel(
+    sum_ref, misfit_ref, gram_at, projection_at, misfit_at, gram_ref, projection_ref, sem
+):
+    members = sum_ref.shape[0]
+    total = sum_ref[...]
+    across = lax.broadcasted_iota(I32, (members, 128), 1)
+    down = lax.broadcasted_iota(I32, (members, 128), 0)
+    gram_ref[...] = total[:, :members]
+    row = jnp.sum(
+        jnp.where(across == down, total[:, members : members + 1], 0.0), axis=0, keepdims=True
+    )
+    projection_ref[...] = row[:, :members]
+    copies = [
+        pltpu.make_async_copy(misfit_ref, misfit_at, sem.at[0]),
+        pltpu.make_async_copy(gram_ref, gram_at, sem.at[1]),
+        pltpu.make_async_copy(projection_ref, projection_at, sem.at[2]),
+    ]
+    for copy in copies:
+        copy.start()
+    for copy in copies:
+        copy.wait()
+
+
+def hbm(count):
+    return [pl.BlockSpec(memory_space=pltpu.HBM)] * count
 
 
 def vmem(count):
@@ -516,14 +605,22 @@
             jax.ShapeDtypeStruct((rows, own), BF),
             jax.ShapeDtypeStruct((near_count, rows, own), BF),
             jax.ShapeDtypeStruct((len(offsets), 2, rows, 128), BF),
-            jax.ShapeDtypeStruct((owners, 3 * each + 8, 128), F32),
+            jax.ShapeDtypeStruct((owners, 3 * each + 16, 128), BF),
         ),
-        in_specs=vmem(7),
+        in_specs=hbm(7),
         out_specs=tuple(vmem(4)),
         scratch_shapes=[
             pltpu.VMEM((rows, own), F32),
             pltpu.VMEM((rows, 128), BF),
-            pltpu.VMEM((owners, 3 * each + 8, 128), F32),
+            pltpu.VMEM((owners, 3 * each + 16, 128), BF),
+            pltpu.VMEM((levels, width, length), F32),
+            pltpu.VMEM((width, length), I32),
+            pltpu.VMEM((1, records), I32),
+            pltpu.VMEM((1, records), I32),
+            pltpu.VMEM((levels, records), F32),
+            pltpu.VMEM((levels, records), F32),
+            pltpu.VMEM((levels, records), F32),
+            dma((7,)),
             dma((near_count,)), dma((near_count,)),
             dma((len(offsets), 2)), dma((len(offsets), 2)),
             dma((owners - 1,)), dma((owners - 1,)),
@@ -536,26 +633,34 @@
         w, inv_var, measured,
     )
 
-    fields, picks, base = pl.pallas_call(
+    final, final_base, picks, base = pl.pallas_call(
         functools.partial(
             steps_kernel, (lat_count, lon_count, offsets, ring, slots, mem_count, records), plans
         ),
         out_shape=(
-            jax.ShapeDtypeStruct((runs, rows, own), BF),
+            jax.ShapeDtypeStruct((local, levels, width, length), BF),
+            jax.ShapeDtypeStruct((levels, width, length), BF),
             jax.ShapeDtypeStruct((mem_count, owners, local, each, 128), BF),
             jax.ShapeDtypeStruct((owners, slots, 128), BF),
         ),
-        in_specs=[pl.BlockSpec(memory_space=pltpu.SMEM)] + vmem(9),
-        out_specs=tuple(vmem(3)),
+        in_specs=[pl.BlockSpec(memory_space=pltpu.SMEM)] + vmem(6) + hbm(3),
+        out_specs=tuple(hbm(2) + vmem(2)),
         scratch_shapes=[
             pltpu.VMEM((runs * rows, total * 128), BF),
             pltpu.VMEM((runs * rows, total * 128), BF),
             pltpu.VMEM((runs * 128, own), BF),
+            pltpu.VMEM(blocks.shape, BF),
+            pltpu.VMEM(pert_table.shape, F32),
+            pltpu.VMEM((1, levels), F32),
+            pltpu.VMEM((runs, levels, width, length), F32),
+            pltpu.VMEM((runs, levels, width, length), BF),
+            dma((3,)),
+            dma((runs,)),
         ],
         compiler_params=limit,
     )(
-        pert_index, main, near, halo, messages, jnp.asarray(blocks, BF), pert_table,
-        base_kh.reshape(1, levels), member_mix, base_mix,
+        pert_index, main, near, halo, messages, member_mix, base_mix,
+        jnp.asarray(blocks, BF), pert_table, base_kh.reshape(1, levels),
     )
 
     sums, misfit = pl.pallas_call(
@@ -564,9 +669,12 @@
             jax.ShapeDtypeStruct((local * mem_count, 128), F32),
             jax.ShapeDtypeStruct((levels, records), F32),
         ),
-        in_specs=vmem(5),
+        in_specs=vmem(3) + hbm(2),
         out_specs=tuple(vmem(2)),
         scratch_shapes=[
+            pltpu.VMEM((levels, records), F32),
+            pltpu.VMEM((levels, records), F32),
+            dma((2,)),
             pltpu.VMEM((mem_count, owners, local, each, 128), BF),
             pltpu.VMEM((owners, slots, 128), BF),
             pltpu.VMEM((mem_count, local * mem_count, 128), F32),
@@ -582,8 +690,21 @@
     )(picks, base, messages, w, measured)
 
     members = local * mem_count
-    final = fields[:, :levels].reshape(runs, levels, width, length)
-    return (final[:local], final[local], sums[:, :members], sums[:, members], misfit.T)
+    gram, projection, misfit = pl.pallas_call(
+        last_kernel,
+        out_shape=(
+            jax.ShapeDtypeStruct((members, members), F32),
+            jax.ShapeDtypeStruct((1, members), F32),
+            jax.ShapeDtypeStruct((levels, records), F32),
+        ),
+        in_specs=vmem(2),
+        out_specs=tuple(hbm(3)),
+        scratch_shapes=[
+            pltpu.VMEM((members, members), F32), pltpu.VMEM((1, members), F32), dma((3,)),
+        ],
+        compiler_params=limit,
+    )(sums, misfit)
+    return (final, final_base, gram, projection.reshape(members), misfit.T)
 
 
 def solution(mesh):

time: 49.4 us -> 46.3 us (0.937)
  local copies, waits for them, and re-layouts: 8.75 us -> 5.4 us
    slice x4 -> x0, local copies, waits for them, and re-layouts: 1.45 us -> none  [the longest x2 0.75 us: on_device(): final[:local]]
    unnamed x29 -> x27, local copies, waits for them, and re-layouts: 6.63 us -> 5.4 us
    pallas_call x0 -> x1, Pallas kernels: none -> 0.67 us  [on_device(): pl.pallas_call(last_kernel, out_shape=(jax.ShapeDtypeStruct((members, mem...]
    squeeze x1 -> x0, local copies, waits for them, and re-layouts: 0.67 us -> none  [on_device(): final[local]]
    pallas_call x1, Pallas kernels: 15.4 us -> 14.8 us  [on_device(): pl.pallas_call(functools.partial(gram_kernel, (mem_count, lat_count, lon_...]
where the time goes in v3:
time: 46.3 us; the launch traced here: 46 us
  Pallas kernels  39.8 us (86%)
  local copies, waits for them, and re-layouts  5.4 us (12%)
  between operations  0.77 us (2%)
    pallas_call x1, Pallas kernels, on_device(): pl.pallas_call(functools.partial(gram_kernel, (mem_count, lat_count, lon_...  14.8 us
    pallas_call x1, Pallas kernels, on_device(): pl.pallas_call(functools.partial(exchange_kernel, (lat_count, lon_count,...  13.1 us
    pallas_call x1, Pallas kernels, on_device(): pl.pallas_call(functools.partial(steps_kernel, (lat_count, lon_count, off...  11.3 us
    unnamed x27, local copies, waits for them, and re-layouts  5.4 us

profile of v3, /device:TPU:0, one launch (start us, length us, event | category | flops | bytes accessed | tf_op | source)
XLA Modules:
  0.0 46.0 jit_solution(9047352864928608440)
XLA Ops:
  0.6 0.0 copy-start.1
  0.6 0.0 copy-start.8
  0.7 0.0 copy-start.9
  0.7 0.0 copy-start.10
  0.7 0.9 %copy.18.mix_ref = bf16[2,100,100]{2,1,0:T(8,128)(2,1)S(1)} copy(bf16[2,100,100]{2,0,1:T(2,128)(2,1)} %param.18) | data formatting | bytes 80000 | tf_op args[5]
  1.5 0.0 copy-done.1
  1.5 0.0 copy-done.8
  1.6 0.0 copy-done.9
  1.6 0.0 copy-done.10
  1.6 0.0 copy-start.2
  1.6 0.9 %copy-done.2 = f32[256,100]{0,1:T(8,128)S(1)} copy-done((f32[256,100]{0,1:T(8,128)S(1)}, f32[256,100]{0,1:T(8,128)}, u32[]{:S(2)}) %copy-start.2) | copy-done | bytes 102424
  2.5 0.9 %copy-done.4 = f32[100,4,128]{2,1,0:T(4,128)S(1)} copy-done((f32[100,4,128]{2,1,0:T(4,128)S(1)}, f32[100,4,128]{2,1,0:T(4,128)}, u32[]{:S(2)}) %copy-start.4) | copy-done | bytes 204824
  3.4 0.9 %copy-done.5 = f32[256,100]{0,1:T(8,128)S(1)} copy-done((f32[256,100]{0,1:T(8,128)S(1)}, f32[256,100]{0,1:T(8,128)}, u32[]{:S(2)}) %copy-start.5) | copy-done | bytes 102424
  4.3 13.1 %shard_map.164 = (bf16[112,512]{1,0:T(8,128)(2,1)S(1)}, bf16[1,112,512]{2,1,0:T(8,128)(2,1)S(1)}, bf16[2,2,112,128]{3,2,1,0:T(8,128)(2,1)S(1)}, bf16[8,64,128]{2,1,0:T(8,128)(2,1)S(1)}) custom-call(f32[100,4,128]{2,1,0:T(4,128)S(1)} %copy-done.4, s32[4,128]{1,0:T(4,128)S(1)} %copy-done.8, s32[1,256]{1,0:T(1,128)S(1)} %bitcast.13, s32[1,256]{1,0:T(1,128)S(1)} %bitcast.14, ...), custom_call_target="tpu_custom_call" | custom-call | tf_op jit(solution)/shard_map/pallas_call | solution.py:602
  17.4 0.0 copy-start.11
  17.4 0.0 copy-start.12
  17.4 0.0 copy-done.6
  17.4 0.6 %copy-done.11 = s32[2]{0:T(128)S(1)} copy-done((s32[2]{0:T(128)S(1)}, s32[2]{0:T(128)}, u32[]{:S(2)}) %copy-start.11) | copy-done | bytes 32
  18.0 0.0 copy-done.12
  18.0 1.1 %copy-done = bf16[3200,128]{1,0:T(8,128)(2,1)S(1)} copy-done((bf16[3200,128]{1,0:T(8,128)(2,1)S(1)}, bf16[3200,128]{1,0:T(8,128)(2,1)}, u32[]{:S(2)}) %copy-start) | copy-done | bytes 819224
  19.2 11.3 %shard_map.165 = (bf16[2,100,4,128]{3,2,1,0:T(4,128)(2,1)}, bf16[100,4,128]{2,1,0:T(4,128)(2,1)}, bf16[4,8,2,16,128]{4,3,2,1,0:T(8,128)(2,1)S(1)}, bf16[8,64,128]{2,1,0:T(8,128)(2,1)S(1)}) custom-call(s32[2]{0:T(128)S(1)} %copy-done.11, bf16[112,512]{1,0:T(8,128)(2,1)S(1)} %get-tuple-element.18.main_ref, ...), custom_call_target="tpu_custom_call" | custom-call | tf_op jit(solution)/shard_map/pallas_call | solution.py:636
  30.5 0.0 copy-done.3
  30.5 14.8 %shard_map.166 = (f32[8,128]{1,0:T(8,128)S(1)}, f32[100,256]{1,0:T(8,128)S(1)}) custom-call(bf16[4,8,2,16,128]{4,3,2,1,0:T(8,128)(2,1)S(1)} %get-tuple-element.24.picks_ref, bf16[8,64,128]{2,1,0:T(8,128)(2,1)S(1)} %get-tuple-element.25.base_ref, bf16[8,64,128]{2,1,0:T(8,128)(2,1)S(1)} %get-tuple-element.21.ids_ref.message_ref, f32[100,256]{1,0:T(8,128)S(1)} %bitcast.9, ...), custom_call_target="tpu_custom_call" | custom-call | tf_op jit(solution)/shard_map/pallas_call | solution.py:666
  45.3 0.7 %shard_map.167 = (f32[8,8]{1,0:T(8,128)}, f32[1,8]{1,0:T(1,128)}, f32[100,256]{1,0:T(8,128)}) custom-call(f32[8,128]{1,0:T(8,128)S(1)} %get-tuple-element.26.sum_ref, f32[100,256]{1,0:T(8,128)S(1)} %get-tuple-element.27.misfit_ref), custom_call_target="tpu_custom_call" | custom-call | tf_op jit(solution)/shard_map/pallas_call | solution.py:693
  (7 shorter events, 0.0 us)
Async XLA Ops:
  0.6 0.9 %copy-start.1 = (f32[256,100]{0,1:T(8,128)S(1)}, f32[256,100]{0,1:T(8,128)}, u32[]{:S(2)}) copy-start(f32[256,100]{0,1:T(8,128)} %param.22) | copy-start | bytes 307204
  0.6 0.9 %copy-start.8 = (s32[4,128]{1,0:T(4,128)S(1)}, s32[4,128]{1,0:T(4,128)}, u32[]{:S(2)}) copy-start(s32[4,128]{1,0:T(4,128)} %refs_1_.1) | copy-start | bytes 6148
  0.7 0.9 %copy-start.9 = (s32[256,1]{0,1:T(1,128)S(1)}, s32[256,1]{0,1:T(1,128)}, u32[]{:S(2)}) copy-start(s32[256,1]{0,1:T(1,128)} %param.20) | copy-start | bytes 3076
  0.7 0.9 %copy-start.10 = (s32[256]{0:T(256)S(1)}, s32[256]{0:T(256)}, u32[]{:S(2)}) copy-start(s32[256]{0:T(256)} %param.21) | copy-start | bytes 3076
  1.6 0.9 %copy-start.2 = (f32[256,100]{0,1:T(8,128)S(1)}, f32[256,100]{0,1:T(8,128)}, u32[]{:S(2)}) copy-start(f32[256,100]{0,1:T(8,128)} %param.24) | copy-start | bytes 307204
  2.5 0.9 %copy-start.4 = (f32[100,4,128]{2,1,0:T(4,128)S(1)}, f32[100,4,128]{2,1,0:T(4,128)}, u32[]{:S(2)}) copy-start(f32[100,4,128]{2,1,0:T(4,128)} %refs_0_.1) | copy-start | bytes 614404
  3.4 0.9 %copy-start.5 = (f32[256,100]{0,1:T(8,128)S(1)}, f32[256,100]{0,1:T(8,128)}, u32[]{:S(2)}) copy-start(f32[256,100]{0,1:T(8,128)} %param.23) | copy-start | bytes 307204
  4.3 13.1 %copy-start.6 = (bf16[100,100]{1,0:T(8,128)(2,1)S(1)}, bf16[100,100]{1,0:T(8,128)(2,1)}, u32[]{:S(2)}) copy-start(bf16[100,100]{1,0:T(8,128)(2,1)} %base_mix_ref.1) | copy-start | bytes 60004
  4.3 13.1 %copy-start.7 = (f32[16,100]{1,0:T(8,128)S(1)}, f32[16,100]{1,0:T(8,128)}, u32[]{:S(2)}) copy-start(f32[16,100]{1,0:T(8,128)} %table_at.1) | copy-start | bytes 19204
  17.4 0.7 %copy-start.11 = (s32[2]{0:T(128)S(1)}, s32[2]{0:T(128)}, u32[]{:S(2)}) copy-start(s32[2]{0:T(128)} %pert_index.1) | copy-start | bytes 28
  17.4 0.7 %copy-start.12 = (f32[100]{0:T(128)S(1)}, f32[100]{0:T(128)}, u32[]{:S(2)}) copy-start(f32[100]{0:T(128)} %param.17) | copy-start | bytes 1204
  18.0 1.1 %copy-start = (bf16[3200,128]{1,0:T(8,128)(2,1)S(1)}, bf16[3200,128]{1,0:T(8,128)(2,1)}, u32[]{:S(2)}) copy-start(bf16[3200,128]{1,0:T(8,128)(2,1)} %constant.2.clone.blocks_at) | copy-start | bytes 2457604
  19.2 11.3 %copy-start.3 = (f32[256,100]{0,1:T(8,128)S(1)}, f32[256,100]{0,1:T(8,128)}, u32[]{:S(2)}) copy-start(f32[256,100]{0,1:T(8,128)} %param.24) | copy-start | bytes 307204
